TPU v7x, 256 devices: a whole 4x4x8 slice. The times are simulated.
256 devices in a mesh: seq: 32 (over x, y, core), tensor: 8 (over z).
Axes of the slice: x: 4, y: 4, z: 8, core: 2. Of those that a mesh axis runs over, the one named last changes fastest.
Arguments:
- hidden_in: bfloat16 [2, 8192, 3584], P(None, 'seq', 'tensor'), may hold values from -6 to 6
- prompt_table: bfloat16 [16, 32, 3584], P(None, None, 'tensor'), may hold values from -6 to 6
- norm_gain: float32 [3584], replicated, may hold values from 0.1 to 1.9
- w_qkv: bfloat16 [3584, 9216], P(None, 'tensor'), may hold values from -4 to 4
- w_out: bfloat16 [7168, 3584], P(('tensor', 'seq')), may hold values from -0.5 to 0.5
- doc_lengths: int32 [2, 16], replicated, may hold values from 1 to 4352, 8192 in all within a row
- doc_tenant: int32 [2, 16], replicated, may hold values from 0 to 15
- prompt_lengths: int32 [2, 16], replicated, may hold values from 1 to 32
Outputs:
- block_out: bfloat16 [2, 8192, 3584], P(None, 'seq', 'tensor')
- tenant_loss: float32 [16], replicated
Inputs may be any that keep to these rules, and one draw needn't show every extreme that they name: `doc_lengths`: each row's 16 lengths sum to 8192, and the longest is exactly 4352.
All inputs are finite; a program needn't handle non-finite values.
Results may differ from a plain program's by a relative error of at most 0.02.
Values may be sent and summed in bfloat16 or wider, within the bound.
A program may use at most 128 MiB of HBM per device.

v0:
```python
import math

import jax
import jax.numpy as jnp
from jax import lax
from jax.sharding import PartitionSpec as P

D = 3584
HEAD_DIM = 128
GROUP = 7
TENANTS = 16
PLEN = 32


THETA = 5000000.0
EPS = 1e-05


def doc_table(lengths, tenants, prompt_len, token_pos):
    starts = jnp.cumsum(lengths) - lengths
    covered = (starts[None, :] <= token_pos[:, None]).astype(jnp.int32)
    doc_ids = jnp.sum(covered, axis=1) - 1
    onehot = (doc_ids[:, None] == jnp.arange(lengths.shape[0], dtype=jnp.int32)[None, :]).astype(
        jnp.int32
    )
    doc_begin = jnp.sum(onehot * starts[None, :], axis=1)
    tenant = jnp.sum(onehot * tenants[None, :], axis=1)
    head_len = jnp.sum(onehot * prompt_len[None, :], axis=1)
    within = token_pos - doc_begin
    return (doc_ids, within, tenant, within < head_len)


def rotate(values_in, within):
    half_dim = values_in.shape[-1] // 2
    inverse_freq = THETA ** (-jnp.arange(half_dim, dtype=jnp.float32) / half_dim)
    angles = within.astype(jnp.float32)[..., None] * inverse_freq
    angles = angles.reshape(within.shape + (1,) * (values_in.ndim - within.ndim - 1) + (half_dim,))
    cosine = jnp.cos(angles)
    sine_part = jnp.sin(angles)
    first_part = values_in[..., :half_dim]
    second = values_in[..., half_dim:]
    return jnp.concatenate(
        [first_part * cosine - second * sine_part, second * cosine + first_part * sine_part],
        axis=-1,
    )


def body(hidden_in, prompt_table, norm_gain, w_qkv, w_out, doc_lengths, doc_tenant, prompt_lengths):
    row_count, shard_len, _ = hidden_in.shape
    longest = (lax.axis_size("seq") // 2 + 1) * shard_len
    first_pos = lax.axis_index("seq") * shard_len
    token_pos = first_pos + jnp.arange(shard_len, dtype=jnp.int32)
    row_table = jax.vmap(doc_table, in_axes=(0, 0, 0, None))
    doc_ids, within, tenant, prompt = row_table(doc_lengths, doc_tenant, prompt_lengths, token_pos)
    flat_table = prompt_table.reshape(TENANTS * PLEN, prompt_table.shape[2])
    table_slot = tenant * PLEN + jnp.minimum(within, PLEN - 1)
    picker = (table_slot[..., None] == jnp.arange(TENANTS * PLEN, dtype=jnp.int32)).astype(
        jnp.bfloat16
    )
    lookup = jnp.einsum(
        "rsk,kd->rsd", picker, flat_table, preferred_element_type=jnp.float32
    ).astype(jnp.bfloat16)
    embedded = jnp.where(prompt[..., None], lookup, hidden_in)
    gathered = lax.all_gather(embedded, "tensor", axis=2, tiled=True)
    wide = gathered.astype(jnp.float32)
    scale = lax.rsqrt(jnp.mean(wide * wide, axis=2, keepdims=True) + EPS)
    normed = (wide * scale * norm_gain).astype(jnp.bfloat16)
    groups = w_qkv.shape[1] // ((GROUP + 2) * HEAD_DIM)
    projected = jnp.einsum("rsd,dc->rsc", normed, w_qkv, preferred_element_type=jnp.float32)
    projected = projected.reshape(row_count, shard_len, groups, GROUP + 2, HEAD_DIM)
    query = rotate(projected[:, :, :, :GROUP], within).astype(jnp.bfloat16)
    key_part = rotate(projected[:, :, :, GROUP], within).astype(jnp.bfloat16)
    value_part = projected[:, :, :, GROUP + 1].astype(jnp.bfloat16)
    key_value = jnp.stack([key_part, value_part], axis=3)
    start_state = (
        jnp.full((row_count, groups, GROUP, shard_len), -1e30, jnp.float32),
        jnp.zeros((row_count, groups, GROUP, shard_len), jnp.float32),
        jnp.zeros((row_count, shard_len, groups, GROUP, HEAD_DIM), jnp.float32),
    )
    pieces = lax.all_gather(key_value, "seq", axis=1, tiled=True)
    piece_start = jnp.int32(0)
    piece_len = pieces.shape[1]
    block_len = math.gcd(piece_len, 512)

    def update_all(carried):

        def one_block(number, inner):
            row_max, totals, weighted = inner
            block_start = number * block_len
            block_kv = lax.dynamic_slice_in_dim(pieces, number * block_len, block_len, 1)
            key_pos = block_start + jnp.arange(block_len, dtype=jnp.int32)
            key_docs = row_table(doc_lengths, doc_tenant, prompt_lengths, key_pos)[0]
            scores = jnp.einsum(
                "rsgjh,rkgh->rgjsk", query, block_kv[:, :, :, 0], preferred_element_type=jnp.float32
            ) * HEAD_DIM ** (-0.5)
            allowed = (doc_ids[:, :, None] == key_docs[:, None, :]) & (
                key_pos[None, None, :] <= token_pos[None, :, None]
            )
            allowed = allowed[:, None, None]
            scores = jnp.where(allowed, scores, -1e30)
            new_max = jnp.maximum(row_max, jnp.max(scores, axis=4))
            weights = jnp.where(allowed, jnp.exp(scores - new_max[..., None]), 0.0)
            rescale = jnp.exp(row_max - new_max)
            totals = totals * rescale + jnp.sum(weights, axis=4)
            summed = jnp.einsum(
                "rgjsk,rkgh->rsgjh",
                weights.astype(jnp.bfloat16),
                block_kv[:, :, :, 1],
                preferred_element_type=jnp.float32,
            )
            weighted = weighted * jnp.transpose(rescale, (0, 3, 1, 2))[..., None] + summed
            return (new_max, totals, weighted)

        return lax.fori_loop(0, piece_len // block_len, one_block, carried)

    useful = (piece_start <= first_pos + shard_len - 1) & (
        piece_start + piece_len > first_pos - longest + 1
    )
    state = lax.cond(useful, update_all, lambda carried: carried, start_state)
    totals = state[1]
    weighted = state[2]
    context = (weighted / jnp.transpose(totals, (0, 3, 1, 2))[..., None]).astype(jnp.bfloat16)
    context = context.reshape(row_count, shard_len, groups * GROUP * HEAD_DIM)
    partial_value = jnp.einsum(
        "rsc,cd->rsd",
        context,
        lax.all_gather(w_out, "seq", axis=0, tiled=True),
        preferred_element_type=jnp.float32,
    )
    delta = lax.psum_scatter(
        partial_value.astype(jnp.bfloat16), "tensor", scatter_dimension=2, tiled=True
    ).astype(jnp.float32)
    block_out = (embedded.astype(jnp.float32) + delta).astype(jnp.bfloat16)
    proxy = jnp.where(prompt, 0.0, jnp.sum(delta * delta, axis=2) / D)
    owner = (tenant[..., None] == jnp.arange(TENANTS, dtype=jnp.int32)).astype(jnp.float32)
    tenant_loss = lax.psum(jnp.sum(owner * proxy[..., None], axis=(0, 1)), ("seq", "tensor"))
    return (block_out, tenant_loss)


def solution(mesh):
    placed = (
        P(None, "seq", "tensor"),
        P(None, None, "tensor"),
        P(),
        P(None, "tensor"),
        P(("tensor", "seq"), None),
        P(),
        P(),
        P(),
    )
    return jax.shard_map(
        body, mesh=mesh, in_specs=placed, out_specs=(P(None, "seq", "tensor"), P()), check_vma=False
    )
```

profile of v0, /device:TPU:1, one launch (start us, length us, event | category | flops | bytes accessed | tf_op | source)
XLA Modules:
  0.0 598.2 jit_solution(4754786545609775363)
XLA Ops:
  13.0 53.0 %all-gather.5.cloned.1.call-done = bf16[2,256,3584]{1,2,0:T(8,128)(2,1)} async-done(((bf16[2,256,448]{1,2,0:T(8,128)(2,1)}), bf16[2,256,3584]{1,2,0:T(8,128)(2,1)}) %all-gather.5.cloned.1.call-update) | async-done | bytes 3670032 | tf_op jit(solution)/shard_map/all_gather | solution.py:64
  68.9 9.2 %fusion.17 = f32[2,256,1152]{1,2,0:T(8,128)S(1)} fusion(bf16[3584,1152]{1,0:T(8,128)(2,1)} %param.15, bf16[2,256,3584]{1,2,0:T(8,128)(2,1)} %all-gather.5.cloned.1.call-done, f32[3584]{0:T(1024)} %param.14, f32[2,256]{1,0:T(2,128)S(1)} %add_rsqrt_fusion), kind=kOutput, calls=%fused_computation.34 | convolution fusion | flops 4235198464 | bytes 14303232 | tf_op jit(solution)/shard_map/rsd,dc->rsc/dot_general | solution.py:69
  80.6 42.9 %all-gather.9.cloned.1.call-done = bf16[32,28,3584]{2,1,0:T(8,128)(2,1)} async-done(((bf16[1,28,3584]{2,1,0:T(8,128)(2,1)}), bf16[32,28,3584]{2,1,0:T(8,128)(2,1)}) %all-gather.9.cloned.1.call-update) | async-done | bytes 6422544 | tf_op jit(solution)/shard_map/all_gather | solution.py:127
  123.5 8.5 %reshape.362 = bf16[896,3584]{1,0:T(8,128)(2,1)} reshape(bf16[32,28,3584]{2,1,0:T(8,128)(2,1)} %all-gather.9.cloned.1.call-done) | data formatting | bytes 12845056
  132.0 57.9 %all-gather.7.cloned.1.call-done = bf16[2,8192,1,2,128]{1,4,3,0,2:T(8,128)(2,1)} async-done(((bf16[2,256,1,2,128]{1,4,3,0,2:T(8,128)(2,1)}), bf16[2,8192,1,2,128]{1,4,3,0,2:T(8,128)(2,1)}) %all-gather.7.cloned.1.call-update) | async-done | bytes 8388624 | tf_op jit(solution)/shard_map/all_gather | solution.py:80
  189.9 262.0 %conditional.1 = (f32[2,1,7,256]{3,2,0,1:T(8,128)}, f32[2,256,1,7,128]{1,4,3,0,2:T(8,128)}) conditional(s32[]{:T(128)} %convert_element_type.87, () %tuple.38, (s32[2,256]{1,0:T(2,128)S(1)}, s32[]{:T(128)}, s32[256]{0:T(256)S(1)}, s32[2,16]{1,0:T(2,128)S(1)}, bf16[2,8192,1,2,128]{1,4,3,0,2:T(8,128)(2,1)}, ...), branch_computations={%region_6.7_spmd, %region_7.14_spmd} | conditional | flops 965483264 | bytes 59900036 | solution.py:119
  190.8 261.1 %while.19 = (s32[]{:T(128)}, f32[2,1,7,256]{3,2,0,1:T(8,128)S(1)}, f32[2,1,7,256]{3,2,0,1:T(8,128)}, f32[2,256,1,7,128]{1,4,3,0,2:T(8,128)}, s32[2,256]{1,0:T(2,...) while((s32[]{:T(128)}, f32[2,1,7,256]{3,2,0,1:T(8,128)S(1)}, ...), condition=%wide.region_13.13_spmd.clone, body=%wide.region_9.12_spmd.clone.sunk | while | flops 965481984 | bytes 58058100 | solution.py:114
  191.3 5.4 fusion.51
  196.7 6.8 %bitcast_add_fusion.5 = f32[2,256,1,7,128]{1,4,3,0,2:T(8,128)} fusion(f32[2,256,1,7,128]{1,4,3,0,2:T(8,128)} %get-tuple-element.416, f32[2,512,256,7]{2,1,3,0:T(8,128)} %get-tuple-element.397, f32[2,7,256]{2,1,0:T(8,128)S(1)} %bitcast.116, pred[2,256,512]{1,2,0:T(8,128)(4,1)S(1)} %compare_and_fusion.2, f32[2,256,7]{1,2,0:T(8,128)S(1)} %get-tuple-element.398, ...), kind=kOutput, calls=%fused_computation.8.clone.1 | convolution fusion | flops 480313344 | bytes 11563017 | tf_op jit(solution)/shard_map/cond/branch_1_fun/while/body/eval_jaxpr/rgjsk,rkgh->rsgjh/dot_general | solution.py:105
  206.5 5.4 fusion.51
  211.9 7.3 %bitcast_add_fusion.5 = f32[2,256,1,7,128]{1,4,3,0,2:T(8,128)} fusion(f32[2,256,1,7,128]{1,4,3,0,2:T(8,128)} %get-tuple-element.416, f32[2,512,256,7]{2,1,3,0:T(8,128)} %get-tuple-element.397, f32[2,7,256]{2,1,0:T(8,128)S(1)} %bitcast.116, pred[2,256,512]{1,2,0:T(8,128)(4,1)S(1)} %compare_and_fusion.2, f32[2,256,7]{1,2,0:T(8,128)S(1)} %get-tuple-element.398, ...), kind=kOutput, calls=%fused_computation.8.clone.1 | convolution fusion | flops 480313344 | bytes 11563017 | tf_op jit(solution)/shard_map/cond/branch_1_fun/while/body/eval_jaxpr/rgjsk,rkgh->rsgjh/dot_general | solution.py:105
  222.9 5.4 fusion.51
  228.3 7.3 %bitcast_add_fusion.5 = f32[2,256,1,7,128]{1,4,3,0,2:T(8,128)} fusion(f32[2,256,1,7,128]{1,4,3,0,2:T(8,128)} %get-tuple-element.416, f32[2,512,256,7]{2,1,3,0:T(8,128)} %get-tuple-element.397, f32[2,7,256]{2,1,0:T(8,128)S(1)} %bitcast.116, pred[2,256,512]{1,2,0:T(8,128)(4,1)S(1)} %compare_and_fusion.2, f32[2,256,7]{1,2,0:T(8,128)S(1)} %get-tuple-element.398, ...), kind=kOutput, calls=%fused_computation.8.clone.1 | convolution fusion | flops 480313344 | bytes 11563017 | tf_op jit(solution)/shard_map/cond/branch_1_fun/while/body/eval_jaxpr/rgjsk,rkgh->rsgjh/dot_general | solution.py:105
  244.7 7.3 %bitcast_add_fusion.5 = f32[2,256,1,7,128]{1,4,3,0,2:T(8,128)} fusion(f32[2,256,1,7,128]{1,4,3,0,2:T(8,128)} %get-tuple-element.416, f32[2,512,256,7]{2,1,3,0:T(8,128)} %get-tuple-element.397, f32[2,7,256]{2,1,0:T(8,128)S(1)} %bitcast.116, pred[2,256,512]{1,2,0:T(8,128)(4,1)S(1)} %compare_and_fusion.2, f32[2,256,7]{1,2,0:T(8,128)S(1)} %get-tuple-element.398, ...), kind=kOutput, calls=%fused_computation.8.clone.1 | convolution fusion | flops 480313344 | bytes 11563017 | tf_op jit(solution)/shard_map/cond/branch_1_fun/while/body/eval_jaxpr/rgjsk,rkgh->rsgjh/dot_general | solution.py:105
  255.7 5.4 fusion.51
  261.1 7.3 %bitcast_add_fusion.5 = f32[2,256,1,7,128]{1,4,3,0,2:T(8,128)} fusion(f32[2,256,1,7,128]{1,4,3,0,2:T(8,128)} %get-tuple-element.416, f32[2,512,256,7]{2,1,3,0:T(8,128)} %get-tuple-element.397, f32[2,7,256]{2,1,0:T(8,128)S(1)} %bitcast.116, pred[2,256,512]{1,2,0:T(8,128)(4,1)S(1)} %compare_and_fusion.2, f32[2,256,7]{1,2,0:T(8,128)S(1)} %get-tuple-element.398, ...), kind=kOutput, calls=%fused_computation.8.clone.1 | convolution fusion | flops 480313344 | bytes 11563017 | tf_op jit(solution)/shard_map/cond/branch_1_fun/while/body/eval_jaxpr/rgjsk,rkgh->rsgjh/dot_general | solution.py:105
  272.1 5.4 fusion.51
  277.5 7.3 %bitcast_add_fusion.5 = f32[2,256,1,7,128]{1,4,3,0,2:T(8,128)} fusion(f32[2,256,1,7,128]{1,4,3,0,2:T(8,128)} %get-tuple-element.416, f32[2,512,256,7]{2,1,3,0:T(8,128)} %get-tuple-element.397, f32[2,7,256]{2,1,0:T(8,128)S(1)} %bitcast.116, pred[2,256,512]{1,2,0:T(8,128)(4,1)S(1)} %compare_and_fusion.2, f32[2,256,7]{1,2,0:T(8,128)S(1)} %get-tuple-element.398, ...), kind=kOutput, calls=%fused_computation.8.clone.1 | convolution fusion | flops 480313344 | bytes 11563017 | tf_op jit(solution)/shard_map/cond/branch_1_fun/while/body/eval_jaxpr/rgjsk,rkgh->rsgjh/dot_general | solution.py:105
  288.5 5.4 fusion.51
  293.9 7.3 %bitcast_add_fusion.5 = f32[2,256,1,7,128]{1,4,3,0,2:T(8,128)} fusion(f32[2,256,1,7,128]{1,4,3,0,2:T(8,128)} %get-tuple-element.416, f32[2,512,256,7]{2,1,3,0:T(8,128)} %get-tuple-element.397, f32[2,7,256]{2,1,0:T(8,128)S(1)} %bitcast.116, pred[2,256,512]{1,2,0:T(8,128)(4,1)S(1)} %compare_and_fusion.2, f32[2,256,7]{1,2,0:T(8,128)S(1)} %get-tuple-element.398, ...), kind=kOutput, calls=%fused_computation.8.clone.1 | convolution fusion | flops 480313344 | bytes 11563017 | tf_op jit(solution)/shard_map/cond/branch_1_fun/while/body/eval_jaxpr/rgjsk,rkgh->rsgjh/dot_general | solution.py:105
  310.3 7.3 %bitcast_add_fusion.5 = f32[2,256,1,7,128]{1,4,3,0,2:T(8,128)} fusion(f32[2,256,1,7,128]{1,4,3,0,2:T(8,128)} %get-tuple-element.416, f32[2,512,256,7]{2,1,3,0:T(8,128)} %get-tuple-element.397, f32[2,7,256]{2,1,0:T(8,128)S(1)} %bitcast.116, pred[2,256,512]{1,2,0:T(8,128)(4,1)S(1)} %compare_and_fusion.2, f32[2,256,7]{1,2,0:T(8,128)S(1)} %get-tuple-element.398, ...), kind=kOutput, calls=%fused_computation.8.clone.1 | convolution fusion | flops 480313344 | bytes 11563017 | tf_op jit(solution)/shard_map/cond/branch_1_fun/while/body/eval_jaxpr/rgjsk,rkgh->rsgjh/dot_general | solution.py:105
  326.6 7.3 %bitcast_add_fusion.5 = f32[2,256,1,7,128]{1,4,3,0,2:T(8,128)} fusion(f32[2,256,1,7,128]{1,4,3,0,2:T(8,128)} %get-tuple-element.416, f32[2,512,256,7]{2,1,3,0:T(8,128)} %get-tuple-element.397, f32[2,7,256]{2,1,0:T(8,128)S(1)} %bitcast.116, pred[2,256,512]{1,2,0:T(8,128)(4,1)S(1)} %compare_and_fusion.2, f32[2,256,7]{1,2,0:T(8,128)S(1)} %get-tuple-element.398, ...), kind=kOutput, calls=%fused_computation.8.clone.1 | convolution fusion | flops 480313344 | bytes 11563017 | tf_op jit(solution)/shard_map/cond/branch_1_fun/while/body/eval_jaxpr/rgjsk,rkgh->rsgjh/dot_general | solution.py:105
  343.0 7.3 %bitcast_add_fusion.5 = f32[2,256,1,7,128]{1,4,3,0,2:T(8,128)} fusion(f32[2,256,1,7,128]{1,4,3,0,2:T(8,128)} %get-tuple-element.416, f32[2,512,256,7]{2,1,3,0:T(8,128)} %get-tuple-element.397, f32[2,7,256]{2,1,0:T(8,128)S(1)} %bitcast.116, pred[2,256,512]{1,2,0:T(8,128)(4,1)S(1)} %compare_and_fusion.2, f32[2,256,7]{1,2,0:T(8,128)S(1)} %get-tuple-element.398, ...), kind=kOutput, calls=%fused_computation.8.clone.1 | convolution fusion | flops 480313344 | bytes 11563017 | tf_op jit(solution)/shard_map/cond/branch_1_fun/while/body/eval_jaxpr/rgjsk,rkgh->rsgjh/dot_general | solution.py:105
  359.4 7.3 %bitcast_add_fusion.5 = f32[2,256,1,7,128]{1,4,3,0,2:T(8,128)} fusion(f32[2,256,1,7,128]{1,4,3,0,2:T(8,128)} %get-tuple-element.416, f32[2,512,256,7]{2,1,3,0:T(8,128)} %get-tuple-element.397, f32[2,7,256]{2,1,0:T(8,128)S(1)} %bitcast.116, pred[2,256,512]{1,2,0:T(8,128)(4,1)S(1)} %compare_and_fusion.2, f32[2,256,7]{1,2,0:T(8,128)S(1)} %get-tuple-element.398, ...), kind=kOutput, calls=%fused_computation.8.clone.1 | convolution fusion | flops 480313344 | bytes 11563017 | tf_op jit(solution)/shard_map/cond/branch_1_fun/while/body/eval_jaxpr/rgjsk,rkgh->rsgjh/dot_general | solution.py:105
  375.8 7.3 %bitcast_add_fusion.5 = f32[2,256,1,7,128]{1,4,3,0,2:T(8,128)} fusion(f32[2,256,1,7,128]{1,4,3,0,2:T(8,128)} %get-tuple-element.416, f32[2,512,256,7]{2,1,3,0:T(8,128)} %get-tuple-element.397, f32[2,7,256]{2,1,0:T(8,128)S(1)} %bitcast.116, pred[2,256,512]{1,2,0:T(8,128)(4,1)S(1)} %compare_and_fusion.2, f32[2,256,7]{1,2,0:T(8,128)S(1)} %get-tuple-element.398, ...), kind=kOutput, calls=%fused_computation.8.clone.1 | convolution fusion | flops 480313344 | bytes 11563017 | tf_op jit(solution)/shard_map/cond/branch_1_fun/while/body/eval_jaxpr/rgjsk,rkgh->rsgjh/dot_general | solution.py:105
  392.2 7.3 %bitcast_add_fusion.5 = f32[2,256,1,7,128]{1,4,3,0,2:T(8,128)} fusion(f32[2,256,1,7,128]{1,4,3,0,2:T(8,128)} %get-tuple-element.416, f32[2,512,256,7]{2,1,3,0:T(8,128)} %get-tuple-element.397, f32[2,7,256]{2,1,0:T(8,128)S(1)} %bitcast.116, pred[2,256,512]{1,2,0:T(8,128)(4,1)S(1)} %compare_and_fusion.2, f32[2,256,7]{1,2,0:T(8,128)S(1)} %get-tuple-element.398, ...), kind=kOutput, calls=%fused_computation.8.clone.1 | convolution fusion | flops 480313344 | bytes 11563017 | tf_op jit(solution)/shard_map/cond/branch_1_fun/while/body/eval_jaxpr/rgjsk,rkgh->rsgjh/dot_general | solution.py:105
  408.6 7.3 %bitcast_add_fusion.5 = f32[2,256,1,7,128]{1,4,3,0,2:T(8,128)} fusion(f32[2,256,1,7,128]{1,4,3,0,2:T(8,128)} %get-tuple-element.416, f32[2,512,256,7]{2,1,3,0:T(8,128)} %get-tuple-element.397, f32[2,7,256]{2,1,0:T(8,128)S(1)} %bitcast.116, pred[2,256,512]{1,2,0:T(8,128)(4,1)S(1)} %compare_and_fusion.2, f32[2,256,7]{1,2,0:T(8,128)S(1)} %get-tuple-element.398, ...), kind=kOutput, calls=%fused_computation.8.clone.1 | convolution fusion | flops 480313344 | bytes 11563017 | tf_op jit(solution)/shard_map/cond/branch_1_fun/while/body/eval_jaxpr/rgjsk,rkgh->rsgjh/dot_general | solution.py:105
  425.0 7.3 %bitcast_add_fusion.5 = f32[2,256,1,7,128]{1,4,3,0,2:T(8,128)} fusion(f32[2,256,1,7,128]{1,4,3,0,2:T(8,128)} %get-tuple-element.416, f32[2,512,256,7]{2,1,3,0:T(8,128)} %get-tuple-element.397, f32[2,7,256]{2,1,0:T(8,128)S(1)} %bitcast.116, pred[2,256,512]{1,2,0:T(8,128)(4,1)S(1)} %compare_and_fusion.2, f32[2,256,7]{1,2,0:T(8,128)S(1)} %get-tuple-element.398, ...), kind=kOutput, calls=%fused_computation.8.clone.1 | convolution fusion | flops 480313344 | bytes 11563017 | tf_op jit(solution)/shard_map/cond/branch_1_fun/while/body/eval_jaxpr/rgjsk,rkgh->rsgjh/dot_general | solution.py:105
  441.4 7.3 %bitcast_add_fusion.5 = f32[2,256,1,7,128]{1,4,3,0,2:T(8,128)} fusion(f32[2,256,1,7,128]{1,4,3,0,2:T(8,128)} %get-tuple-element.416, f32[2,512,256,7]{2,1,3,0:T(8,128)} %get-tuple-element.397, f32[2,7,256]{2,1,0:T(8,128)S(1)} %bitcast.116, pred[2,256,512]{1,2,0:T(8,128)(4,1)S(1)} %compare_and_fusion.2, f32[2,256,7]{1,2,0:T(8,128)S(1)} %get-tuple-element.398, ...), kind=kOutput, calls=%fused_computation.8.clone.1 | convolution fusion | flops 480313344 | bytes 11563017 | tf_op jit(solution)/shard_map/cond/branch_1_fun/while/body/eval_jaxpr/rgjsk,rkgh->rsgjh/dot_general | solution.py:105
  453.6 9.7 %fusion.24 = bf16[2,256,3584]{1,2,0:T(8,128)(2,1)} fusion(bf16[2,256,896]{1,2,0:T(8,128)(2,1)S(1)} %bitcast.121, bf16[896,3584]{1,0:T(8,128)(2,1)} %reshape.362), kind=kOutput, calls=%fused_computation.41 | convolution fusion | flops 3290169344 | bytes 11010048 | tf_op jit(solution)/shard_map/rsc,cd->rsd/dot_general | solution.py:124
  463.3 49.9 %reduce-scatter.2.cloned.1.call-done = bf16[2,256,448]{1,2,0:T(8,128)(2,1)} async-done(((bf16[2,256,3584]{1,2,0:T(8,128)(2,1)}), bf16[2,256,448]{1,2,0:T(8,128)(2,1)}) %reduce-scatter.2.cloned.1.call-update) | async-done | bytes 458768 | tf_op jit(solution)/shard_map/reduce_scatter | solution.py:130
  515.3 76.4 %psum.7 = f32[16]{0:T(128)} all-reduce(f32[16]{0:T(128)S(1)} %select_reduce_fusion), channel_id=1, replica_groups=mesh['seq'=32,'tensor'=8] {'seq','tensor'}, use_global_device_ids=true, to_apply=%region_17.18 | all-reduce | flops 16 | bytes 128 | tf_op jit(solution)/shard_map/psum | solution.py:136
  (232 shorter events, 127.8 us)
Async XLA Ops:
  7.2 2.6 copy-start
  7.2 58.9 %all-gather.5.cloned.1.call-start = ((), (), s32[]{:S(2)}) async-start(), calls=%async_computation.1 | async-start | bytes 4128768 | tf_op jit(solution)/shard_map/all_gather | solution.py:64
  12.2 111.3 %all-gather.9.cloned.1.call-start = ((), (), s32[]{:S(2)}) async-start(), calls=%async_computation.4 | async-start | bytes 7569408 | tf_op jit(solution)/shard_map/all_gather | solution.py:127
  13.0 176.9 %all-gather.7.cloned.1.call-start = ((), (), s32[]{:S(2)}) async-start(), calls=%async_computation.2 | async-start | bytes 8650752 | tf_op jit(solution)/shard_map/all_gather | solution.py:80
  79.5 433.7 %reduce-scatter.2.cloned.1.call-start = ((), (), s32[]{:S(2)}) async-start(), calls=%async_computation.3 | async-start | bytes 4128768 | tf_op jit(solution)/shard_map/reduce_scatter | solution.py:130
  80.6 109.3 %copy-start.3 = (s32[2,16]{1,0:T(2,128)S(1)}, s32[2,16]{1,0:T(2,128)}, u32[]{:S(2)}) copy-start(s32[2,16]{1,0:T(2,128)} %param.17) | copy-start | bytes 388
  196.7 6.8 %copy-start.1 = (f32[2,512,256,7]{2,1,3,0:T(8,128)S(1)}, f32[2,512,256,7]{2,1,3,0:T(8,128)}, u32[]{:S(2)}) copy-start(f32[2,512,256,7]{2,1,3,0:T(8,128)} %get-tuple-element.397) | copy-start | bytes 22020100 | tf_op jit(solution)/shard_map/cond/branch_1_fun/while
  211.9 7.3 %copy-start.1 = (f32[2,512,256,7]{2,1,3,0:T(8,128)S(1)}, f32[2,512,256,7]{2,1,3,0:T(8,128)}, u32[]{:S(2)}) copy-start(f32[2,512,256,7]{2,1,3,0:T(8,128)} %get-tuple-element.397) | copy-start | bytes 22020100 | tf_op jit(solution)/shard_map/cond/branch_1_fun/while
  228.3 7.3 %copy-start.1 = (f32[2,512,256,7]{2,1,3,0:T(8,128)S(1)}, f32[2,512,256,7]{2,1,3,0:T(8,128)}, u32[]{:S(2)}) copy-start(f32[2,512,256,7]{2,1,3,0:T(8,128)} %get-tuple-element.397) | copy-start | bytes 22020100 | tf_op jit(solution)/shard_map/cond/branch_1_fun/while
  244.7 7.3 %copy-start.1 = (f32[2,512,256,7]{2,1,3,0:T(8,128)S(1)}, f32[2,512,256,7]{2,1,3,0:T(8,128)}, u32[]{:S(2)}) copy-start(f32[2,512,256,7]{2,1,3,0:T(8,128)} %get-tuple-element.397) | copy-start | bytes 22020100 | tf_op jit(solution)/shard_map/cond/branch_1_fun/while
  261.1 7.3 %copy-start.1 = (f32[2,512,256,7]{2,1,3,0:T(8,128)S(1)}, f32[2,512,256,7]{2,1,3,0:T(8,128)}, u32[]{:S(2)}) copy-start(f32[2,512,256,7]{2,1,3,0:T(8,128)} %get-tuple-element.397) | copy-start | bytes 22020100 | tf_op jit(solution)/shard_map/cond/branch_1_fun/while
  277.5 7.3 %copy-start.1 = (f32[2,512,256,7]{2,1,3,0:T(8,128)S(1)}, f32[2,512,256,7]{2,1,3,0:T(8,128)}, u32[]{:S(2)}) copy-start(f32[2,512,256,7]{2,1,3,0:T(8,128)} %get-tuple-element.397) | copy-start | bytes 22020100 | tf_op jit(solution)/shard_map/cond/branch_1_fun/while
  293.8 7.3 %copy-start.1 = (f32[2,512,256,7]{2,1,3,0:T(8,128)S(1)}, f32[2,512,256,7]{2,1,3,0:T(8,128)}, u32[]{:S(2)}) copy-start(f32[2,512,256,7]{2,1,3,0:T(8,128)} %get-tuple-element.397) | copy-start | bytes 22020100 | tf_op jit(solution)/shard_map/cond/branch_1_fun/while
  310.2 7.3 %copy-start.1 = (f32[2,512,256,7]{2,1,3,0:T(8,128)S(1)}, f32[2,512,256,7]{2,1,3,0:T(8,128)}, u32[]{:S(2)}) copy-start(f32[2,512,256,7]{2,1,3,0:T(8,128)} %get-tuple-element.397) | copy-start | bytes 22020100 | tf_op jit(solution)/shard_map/cond/branch_1_fun/while
  326.6 7.3 %copy-start.1 = (f32[2,512,256,7]{2,1,3,0:T(8,128)S(1)}, f32[2,512,256,7]{2,1,3,0:T(8,128)}, u32[]{:S(2)}) copy-start(f32[2,512,256,7]{2,1,3,0:T(8,128)} %get-tuple-element.397) | copy-start | bytes 22020100 | tf_op jit(solution)/shard_map/cond/branch_1_fun/while
  343.0 7.3 %copy-start.1 = (f32[2,512,256,7]{2,1,3,0:T(8,128)S(1)}, f32[2,512,256,7]{2,1,3,0:T(8,128)}, u32[]{:S(2)}) copy-start(f32[2,512,256,7]{2,1,3,0:T(8,128)} %get-tuple-element.397) | copy-start | bytes 22020100 | tf_op jit(solution)/shard_map/cond/branch_1_fun/while
  359.4 7.3 %copy-start.1 = (f32[2,512,256,7]{2,1,3,0:T(8,128)S(1)}, f32[2,512,256,7]{2,1,3,0:T(8,128)}, u32[]{:S(2)}) copy-start(f32[2,512,256,7]{2,1,3,0:T(8,128)} %get-tuple-element.397) | copy-start | bytes 22020100 | tf_op jit(solution)/shard_map/cond/branch_1_fun/while
  375.8 7.3 %copy-start.1 = (f32[2,512,256,7]{2,1,3,0:T(8,128)S(1)}, f32[2,512,256,7]{2,1,3,0:T(8,128)}, u32[]{:S(2)}) copy-start(f32[2,512,256,7]{2,1,3,0:T(8,128)} %get-tuple-element.397) | copy-start | bytes 22020100 | tf_op jit(solution)/shard_map/cond/branch_1_fun/while
  392.2 7.3 %copy-start.1 = (f32[2,512,256,7]{2,1,3,0:T(8,128)S(1)}, f32[2,512,256,7]{2,1,3,0:T(8,128)}, u32[]{:S(2)}) copy-start(f32[2,512,256,7]{2,1,3,0:T(8,128)} %get-tuple-element.397) | copy-start | bytes 22020100 | tf_op jit(solution)/shard_map/cond/branch_1_fun/while
  408.6 7.3 %copy-start.1 = (f32[2,512,256,7]{2,1,3,0:T(8,128)S(1)}, f32[2,512,256,7]{2,1,3,0:T(8,128)}, u32[]{:S(2)}) copy-start(f32[2,512,256,7]{2,1,3,0:T(8,128)} %get-tuple-element.397) | copy-start | bytes 22020100 | tf_op jit(solution)/shard_map/cond/branch_1_fun/while
  425.0 7.3 %copy-start.1 = (f32[2,512,256,7]{2,1,3,0:T(8,128)S(1)}, f32[2,512,256,7]{2,1,3,0:T(8,128)}, u32[]{:S(2)}) copy-start(f32[2,512,256,7]{2,1,3,0:T(8,128)} %get-tuple-element.397) | copy-start | bytes 22020100 | tf_op jit(solution)/shard_map/cond/branch_1_fun/while
  441.4 7.3 %copy-start.1 = (f32[2,512,256,7]{2,1,3,0:T(8,128)S(1)}, f32[2,512,256,7]{2,1,3,0:T(8,128)}, u32[]{:S(2)}) copy-start(f32[2,512,256,7]{2,1,3,0:T(8,128)} %get-tuple-element.397) | copy-start | bytes 22020100 | tf_op jit(solution)/shard_map/cond/branch_1_fun/while
  453.6 59.6 %copy-start.2 = (bf16[2,256,448]{1,2,0:T(8,128)(2,1)S(1)}, bf16[2,256,448]{1,2,0:T(8,128)(2,1)}, u32[]{:S(2)}) copy-start(bf16[2,256,448]{1,2,0:T(8,128)(2,1)} %fusion.30) | copy-start | bytes 1376260
Sparse Core Ops, SparseCore 0:
  12.3 53.6 all-gather.4
  68.6 54.8 all-gather.8
  126.0 63.8 all-gather.6
  463.4 49.7 reduce-scatter.1
where the time goes:
time: 600 us; the launch traced here: 598 us
  matrix products  223 us (37%)
  waiting for transfers between devices  205 us (34%)
  blocking collectives  76.4 us (13%)
  other arithmetic  69.8 us (12%)
  between operations  13.9 us (2%)
  local copies, waits for them, and re-layouts  9.23 us (2%)
    dot_general x16, matrix products, one_block(): jnp.einsum('rgjsk,rkgh->rsgjh', weights.astype(jnp.bfloat16), block_kv[:,...  116 us
    dot_general x16, matrix products, one_block(): jnp.einsum('rsgjh,rkgh->rgjsk', query, block_kv[:, :, :, 0], preferred_el...  86 us
    psum x1, blocking collectives, body(): lax.psum(jnp.sum(owner * proxy[..., None], axis=(0, 1)), ('seq', 'tensor'))  76.4 us
    all_gather x1, waiting for transfers between devices, body(): pieces = lax.all_gather(key_value, 'seq', axis=1, tiled=True)  57.9 us
    all_gather x1, waiting for transfers between devices, body(): gathered = lax.all_gather(embedded, 'tensor', axis=2, tiled=True)  53 us
    reduce_scatter x1, waiting for transfers between devices, body(): lax.psum_scatter(partial_value.astype(jnp.bfloat16), 'tensor', scatter_di...  49.9 us
    all_gather x1, waiting for transfers between devices, body(): lax.all_gather(w_out, 'seq', axis=0, tiled=True)  42.9 us
    reduce_sum x16, other arithmetic, one_block(): totals = totals * rescale + jnp.sum(weights, axis=4)  29.5 us
  transfers between devices with their start and end apart: 4, of which 4 were waited for; matrix products, arithmetic and copies ran while one was open for 4% of the time, Pallas kernels for 0%

commit v1 on v0

v1 whole, which is shorter than its diff:
```python
import functools

import jax
import jax.numpy as jnp
import numpy as np
from jax import lax
from jax.experimental import pallas as pl
from jax.experimental.pallas import tpu as pltpu
from jax.sharding import PartitionSpec as P

D = 3584
HEAD_DIM = 128
GROUP = 7
TENANTS = 16
PLEN = 32
THETA = 5000000.0
EPS = 1e-05

SEQ = 32
RING = 8
POS = 256
FEAT = 448
HALF = POS // 2
WIDE = 2 * FEAT
SUB = HALF // 2
COLS = (GROUP + 2) * HEAD_DIM
SHARD = 28
SLOT = 32
DEPTH = SEQ * SLOT
WINDOW = 9
QSCALE = HEAD_DIM**-0.5 * 1.4426950408889634
LOW = -1e30
MESH = pl.DeviceIdType.MESH
F32 = jnp.float32
BF16 = jnp.bfloat16


def dot(a, b):
    return jnp.dot(a, b, preferred_element_type=F32)


def place():
    return lax.axis_index("seq"), lax.axis_index("tensor")


def greet(peers):
    barrier = pltpu.get_barrier_semaphore()
    for peer in peers:
        pl.semaphore_signal(barrier, inc=1, device_id=peer, device_id_type=MESH)
    pl.semaphore_wait(barrier, len(peers))


def ring_peers():
    s, z = place()
    return [(s, lax.rem(z + 1, RING)), (s, lax.rem(z + RING - 1, RING))]


def push(src, dst, send, recv, peer):
    return pltpu.make_async_remote_copy(
        src_ref=src, dst_ref=dst, send_sem=send, recv_sem=recv, device_id=peer, device_id_type=MESH
    )


def unpack(x):
    return jnp.concatenate([x[:, :FEAT], x[:, FEAT:]], axis=0)


def pack(x):
    return jnp.concatenate([x[:HALF], x[HALF:]], axis=1)


def feature_steps(x, buf, send, recv, absorb):
    s, z = place()
    peers = ring_peers()

    def moved(way, hop, sub, mine):
        step = 1 if way == 0 else RING - 1
        origin = lax.rem(z + (RING - step) * (hop - 1 if mine else hop), RING)
        rows = pl.ds(sub * SUB, SUB)
        src = x.at[rows] if mine and hop == 1 else buf.at[origin, rows]
        index = (way, hop - 1, sub)
        return push(src, buf.at[origin, rows], send.at[index], recv.at[index], peers[way])

    sent = []

    def go(way, hop, sub):
        if hop == 4 and sub != way:
            return
        copy = moved(way, hop, sub, True)
        copy.start()
        sent.append(copy)

    for sub in range(2):
        for way in range(2):
            go(way, 1, sub)
    yield
    absorb(x[...], z)
    yield
    for hop in range(1, 4):
        for sub in range(2):
            for way in range(2):
                moved(way, hop, sub, False).wait_recv()
                go(way, hop + 1, sub)
            yield
        absorb(buf[lax.rem(z + RING - hop, RING)], lax.rem(z + RING - hop, RING))
        yield
        absorb(buf[lax.rem(z + hop, RING)], lax.rem(z + hop, RING))
        yield
    for way in range(2):
        moved(way, 4, way, False).wait_recv()
    yield
    absorb(buf[lax.rem(z + 4, RING)], lax.rem(z + 4, RING))
    yield
    for copy in sent:
        copy.wait_send()


class Projection:
    def __init__(self, gain, w, cos, sin, wbuf, wsem, acc, ssq):
        self.gain, self.w, self.cos, self.sin = gain, w, cos, sin
        self.wbuf, self.wsem, self.acc, self.ssq = wbuf, wsem, acc, ssq

    def fetch(self):
        z = place()[1]
        for away in (0, 7, 1, 6, 2, 5, 3, 4):
            self.copy(lax.rem(z + away, RING)).start()

    def copy(self, origin):
        return pltpu.make_async_copy(
            self.w.at[pl.ds(origin * FEAT, FEAT)], self.wbuf.at[origin], self.wsem.at[origin]
        )

    def clear(self):
        self.acc[...] = jnp.zeros_like(self.acc)
        self.ssq[...] = jnp.zeros_like(self.ssq)

    def absorb(self, x, origin):
        self.copy(origin).wait()
        wide = unpack(x).astype(F32)
        self.ssq[...] += jnp.sum(wide * wide, axis=1, keepdims=True)
        scaled = (wide * self.gain[origin]).astype(BF16)
        self.acc[...] += dot(scaled, self.wbuf[origin])

    def finish(self, q, kv):
        scale = lax.rsqrt(self.ssq[:, :1] / D + EPS)
        cos, sin = self.cos[...], self.sin[...]

        def rotated(n):
            part = self.acc[:, n * HEAD_DIM : (n + 1) * HEAD_DIM] * scale
            return part * cos + pltpu.roll(part, HEAD_DIM // 2, 1) * sin

        for n in range(GROUP):
            q[n] = (rotated(n) * QSCALE).astype(BF16)
        kv[:HEAD_DIM] = rotated(GROUP).T.astype(BF16)
        value = (self.acc[:, (GROUP + 1) * HEAD_DIM :] * scale).astype(BF16)
        kv[HEAD_DIM:] = pack(value)


def plane_peers():
    s, z = place()
    x, y, c = s // 8, lax.rem(s // 2, 4), lax.rem(s, 2)

    def at(a, b):
        dx, dy = a * (1 - c) + b * c, a * c + b * (1 - c)
        return lax.rem(x + dx, 4) * 8 + lax.rem(y + dy, 4) * 2 + c

    return at, [(at(1, 0), z), (at(3, 0), z)], [(at(0, 1), z), (at(0, 3), z)], (s + 1 - 2 * c, z)


def key_steps(own, everyone, send, recv, local):
    at, first, second, sibling = plane_peers()
    s, _ = place()
    sent = []
    halves = (pl.ds(0, HALF), pl.ds(HALF, HALF))
    back = (3, 1)

    def give(slot, rows, index, peer, src=None):
        ref = everyone.at[slot, rows] if rows is not None else everyone.at[slot]
        return push(ref if src is None else src, ref, send.at[index], recv.at[index], peer)

    def go(*args, **kwargs):
        copy = give(*args, **kwargs)
        copy.start()
        sent.append(copy)

    keep = pltpu.make_async_copy(own, everyone.at[s], local)
    keep.start()
    for way in range(2):
        go(s, None, way, first[way], src=own)
    for way in range(2):
        go(s, None, 4 + way, second[way], src=own)
    go(s, None, 20, sibling, src=own)
    yield

    def spread(a, slot):
        for way in range(2):
            go(slot, None, 4 + 4 * a + way, second[way])
        go(slot, None, 20 + 4 * a, sibling)

    for way in range(2):
        slot = at(back[way], 0)
        give(slot, None, way, first[way]).wait_recv()
        go(slot, halves[way], 2 + way, first[way])
        spread(back[way], slot)
    yield
    slot = at(2, 0)
    for way in range(2):
        give(slot, halves[way], 2 + way, first[way]).wait_recv()
    spread(2, slot)
    yield
    for a in (0, 3, 1, 2):
        for way in range(2):
            slot = at(a, back[way])
            give(slot, None, 4 + 4 * a + way, second[way]).wait_recv()
            go(slot, halves[way], 6 + 4 * a + way, second[way])
            go(slot, None, 20 + 4 * a + back[way], sibling)
        yield
    for a in (0, 3, 1, 2):
        slot = at(a, 2)
        for way in range(2):
            give(slot, halves[way], 6 + 4 * a + way, second[way]).wait_recv()
        go(slot, None, 20 + 4 * a + 2, sibling)
        yield
    c = lax.rem(s, 2)
    x, y = s // 8, lax.rem(s // 2, 4)
    for a in range(4):
        for b in range(4):
            dx, dy = a * c + b * (1 - c), a * (1 - c) + b * c
            slot = lax.rem(x + dx, 4) * 8 + lax.rem(y + dy, 4) * 2 + 1 - c
            give(slot, None, 20 + 4 * a + b, sibling).wait_recv()
    keep.wait()
    for copy in sent:
        copy.wait_send()
    yield


KEY_SEMS = 36


def attend(step, q, kv, begin, acc, top):
    s, _ = place()
    last = s - 2 * step
    low = jnp.maximum(last - 1, 0)
    key_pos = low * POS + lax.broadcasted_iota(jnp.int32, (POS, 2 * POS), 1)
    query_pos = s * POS + lax.broadcasted_iota(jnp.int32, (POS, 2 * POS), 0)
    allowed = (key_pos >= begin) & (key_pos <= jnp.minimum(query_pos, last * POS + POS - 1))
    bias = jnp.where(allowed, 0.0, LOW)
    blocks = kv[pl.ds(low, 2)]
    keys = jnp.concatenate([blocks[0, :HEAD_DIM], blocks[1, :HEAD_DIM]], axis=1)
    values = [blocks[n, HEAD_DIM:, m * HEAD_DIM : (m + 1) * HEAD_DIM] for n in (0, 1) for m in (0, 1)]
    values = jnp.concatenate(values, axis=0)
    values = jnp.concatenate([values, jnp.ones_like(values)], axis=1)
    for n in range(GROUP):
        scores = dot(q[n], keys) + bias
        old = top[n]
        new = jnp.maximum(old, jnp.max(scores, axis=1, keepdims=True))
        weights = jnp.exp2(scores - jnp.concatenate([new] * 4, axis=1)).astype(BF16)
        rescale = jnp.exp2(old - new)
        acc[n] = acc[n] * jnp.concatenate([rescale] * 2, axis=1) + dot(weights, values)
        top[n] = new


def start_attend(acc, top):
    acc[...] = jnp.zeros_like(acc)
    top[...] = jnp.full_like(top, LOW)


def finish_attend(acc, ctx):
    for n in range(GROUP):
        both = acc[n]
        ctx[:, n * HEAD_DIM : (n + 1) * HEAD_DIM] = (both[:, :HEAD_DIM] / both[:, HEAD_DIM:]).astype(BF16)


class Sums:
    def __init__(self, w, wbuf, wsem, out, came, send, recv):
        self.w, self.wbuf, self.wsem = w, wbuf, wsem
        self.out, self.came, self.send, self.recv = out, came, send, recv
        self.peers = ring_peers()
        self.sent = []

    def copy(self, owner):
        return pltpu.make_async_copy(self.w.at[:, owner], self.wbuf.at[owner], self.wsem.at[owner])

    def fetch(self):
        z = place()[1]
        for away in (4, 3, 5, 2, 6, 1, 7, 0):
            self.copy(lax.rem(z + away, RING)).start()

    def part(self, owner):
        self.copy(owner).wait()
        return pack(dot(self.ctx, self.wbuf[owner].reshape(DEPTH, FEAT)))

    def move(self, way, k, sub):
        rows = pl.ds(sub * SUB, SUB)
        index = (way, k, sub)
        return push(
            self.out.at[way, k, rows], self.came.at[way, k, rows],
            self.send.at[index], self.recv.at[index], self.peers[way],
        )

    def ship(self, way, k, sub, value):
        self.out[way, k, pl.ds(sub * SUB, SUB)] = value.astype(BF16)
        copy = self.move(way, k, sub)
        copy.start()
        self.sent.append(copy)

    def arrived(self, way, k, sub):
        self.move(way, k, sub).wait_recv()
        return self.came[way, k, pl.ds(sub * SUB, SUB)].astype(F32)

    def steps(self, ctx, perm):
        z = place()[1]
        self.ctx = dot(ctx[...], perm[...]).astype(BF16)
        value = self.part(lax.rem(z + 4, RING))
        for way in range(2):
            self.ship(way, 0, way, value[way * SUB : (way + 1) * SUB])
        yield
        for k in range(1, 4):
            value = [self.part(lax.rem(z + 4 - k, RING)), self.part(lax.rem(z + 4 + k, RING))]
            for turn in range(2):
                for way in range(2):
                    sub = turn ^ way if k == 1 else turn
                    piece = value[way][sub * SUB : (sub + 1) * SUB]
                    if k > 1 or sub == way:
                        piece = piece + self.arrived(way, k - 1, sub)
                    self.ship(way, k, sub, piece)
                yield
        value = self.part(z)
        got = []
        for sub in range(2):
            piece = value[sub * SUB : (sub + 1) * SUB]
            for way in range(2):
                piece = piece + self.arrived(way, 3, sub)
            got.append(piece)
        self.delta = jnp.concatenate(got, axis=0)
        for copy in self.sent:
            copy.wait_send()
        yield


def emit(sums, emb, owner, out, loss):
    delta = unpack(sums.delta)
    out[...] = (unpack(emb[...]).astype(F32) + delta).astype(BF16)
    proxy = jnp.sum(delta * delta, axis=1, keepdims=True) / D
    lanes = lax.broadcasted_iota(jnp.int32, (POS, HEAD_DIM), 1)
    total = jnp.sum(jnp.where(owner[...] == lanes, proxy, 0.0), axis=0, keepdims=True)
    loss[...] = jnp.broadcast_to(total, loss.shape)


def loss_groups():
    s, z = place()
    x, y, c = s // 8, lax.rem(s // 2, 4), lax.rem(s, 2)
    xc = x * 2 + c
    return [
        (z, 8, lambda n: (s, n)),
        (xc, 8, lambda n: ((n // 2) * 8 + y * 2 + lax.rem(n, 2), z)),
        (y, 4, lambda n: (x * 8 + n * 2 + c, z)),
    ]


def loss_peers():
    return [who(lax.rem(me + j, n)) for me, n, who in loss_groups() for j in range(1, n)]


def loss_total(value, slots, send, recv):
    for stage, (me, n, who) in enumerate(loss_groups()):
        slots[stage, me] = value
        sent = []
        for j in range(1, n):
            ref = slots.at[stage, me]
            copy = push(ref, ref, send.at[stage, j], recv.at[stage, j], who(lax.rem(me + j, n)))
            copy.start()
            sent.append(copy)
        for j in range(1, n):
            ref = slots.at[stage, lax.rem(me + n - j, n)]
            push(ref, ref, send.at[stage, j], recv.at[stage, j], who(lax.rem(me + j, n))).wait_recv()
        value = slots[stage, 0]
        for j in range(1, n):
            value = value + slots[stage, j]
        for copy in sent:
            copy.wait_send()
    return value


def alternate(*many):
    many = list(many)
    while many:
        for one in list(many):
            try:
                next(one)
            except StopIteration:
                many.remove(one)


RING_SEMS = pltpu.SemaphoreType.DMA((2, 4, 2))
FEATURE_SCRATCH = [
    pltpu.VMEM((RING, HALF, WIDE), BF16),
    pltpu.VMEM((RING, FEAT, COLS), BF16),
    pltpu.SemaphoreType.DMA((RING,)),
    pltpu.VMEM((POS, COLS), F32),
    pltpu.VMEM((POS, HEAD_DIM), F32),
    RING_SEMS,
    RING_SEMS,
]
KEY_SCRATCH = [
    pltpu.SemaphoreType.DMA((KEY_SEMS,)),
    pltpu.SemaphoreType.DMA((KEY_SEMS,)),
    pltpu.SemaphoreType.DMA,
]
SUM_SCRATCH = [
    pltpu.VMEM((RING, SEQ, SLOT, FEAT), BF16),
    pltpu.SemaphoreType.DMA((RING,)),
    pltpu.VMEM((2, 4, HALF, WIDE), BF16),
    pltpu.VMEM((2, 4, HALF, WIDE), BF16),
    RING_SEMS,
    RING_SEMS,
]
ATTEND_SCRATCH = [
    pltpu.VMEM((GROUP, POS, 2 * HEAD_DIM), F32),
    pltpu.VMEM((GROUP, POS, HEAD_DIM), F32),
]
VM = pl.BlockSpec(memory_space=pltpu.VMEM)
ANY = pl.BlockSpec(memory_space=pl.ANY)
Q_SHAPE = jax.ShapeDtypeStruct((GROUP, POS, HEAD_DIM), BF16)
KV_SHAPE = jax.ShapeDtypeStruct((POS, 2 * HEAD_DIM), BF16)
KEYS_SHAPE = jax.ShapeDtypeStruct((SEQ, POS, 2 * HEAD_DIM), BF16)
CTX_SHAPE = jax.ShapeDtypeStruct((POS, GROUP * HEAD_DIM), BF16)
OUT_SHAPE = jax.ShapeDtypeStruct((POS, FEAT), BF16)
LOSS_SHAPE = jax.ShapeDtypeStruct((8, HEAD_DIM), F32)


def project_kernel(x, gain, w, cos, sin, q, kv, buf, wbuf, wsem, acc, ssq, send, recv):
    proj = Projection(gain, w, cos, sin, wbuf, wsem, acc, ssq)
    proj.fetch()
    greet(ring_peers())
    proj.clear()
    alternate(feature_steps(x, buf, send, recv, proj.absorb))
    proj.finish(q, kv)


def project_keys_kernel(
    x, gain, w, cos, sin, own, q, kv, everyone,
    buf, wbuf, wsem, acc, ssq, send, recv, ksend, krecv, klocal,
):
    proj = Projection(gain, w, cos, sin, wbuf, wsem, acc, ssq)
    proj.fetch()
    _, first, second, sibling = plane_peers()
    greet(ring_peers() + first + second + [sibling])
    proj.clear()
    alternate(
        feature_steps(x, buf, send, recv, proj.absorb),
        key_steps(own, everyone, ksend, krecv, klocal),
    )
    proj.finish(q, kv)


def keys_kernel(own, everyone, ksend, krecv, klocal):
    _, first, second, sibling = plane_peers()
    greet(first + second + [sibling])
    alternate(key_steps(own, everyone, ksend, krecv, klocal))


def attend_kernel(count, q0, q1, kv0, kv1, begin0, begin1, ctx0, ctx1, acc, top):
    for row, (q, kv, begin, ctx) in enumerate(((q0, kv0, begin0, ctx0), (q1, kv1, begin1, ctx1))):
        start_attend(acc, top)

        def step(n, carry, q=q, kv=kv, begin=begin):
            attend(n, q, kv, begin[...], acc, top)
            return carry

        lax.fori_loop(0, count[row], step, 0)
        finish_attend(acc, ctx)


def sums_kernel(ctx, perm, w, emb, owner, out, loss, *scratch):
    sums = Sums(w, *scratch)
    sums.fetch()
    greet(sums.peers)
    alternate(sums.steps(ctx, perm))
    emit(sums, emb, owner, out, loss)


def last_kernel(ctx, perm, w, emb, owner, other, out, loss, *scratch):
    *scratch, slots, lsend, lrecv = scratch
    sums = Sums(w, *scratch)
    sums.fetch()
    greet(loss_peers())
    alternate(sums.steps(ctx, perm))
    emit(sums, emb, owner, out, loss)
    loss[...] = loss_total(loss[...] + other[...], slots, lsend, lrecv)


def call(kernel, ident, out_shape, in_specs, out_specs, scratch, mib, flops):
    return pl.pallas_call(
        kernel,
        out_shape=out_shape,
        in_specs=in_specs,
        out_specs=out_specs,
        scratch_shapes=scratch,
        compiler_params=pltpu.CompilerParams(
            collective_id=ident,
            has_side_effects=ident is not None,
            vmem_limit_bytes=mib * 2**20,
        ),
        cost_estimate=pl.CostEstimate(flops=flops, bytes_accessed=2**23, transcendentals=0),
        name=kernel.__name__,
    )


def doc_table(lengths, tenants, prompt_len, token_pos):
    starts = jnp.cumsum(lengths) - lengths
    covered = (starts[None, :] <= token_pos[:, None]).astype(jnp.int32)
    doc_ids = jnp.sum(covered, axis=1) - 1
    onehot = (doc_ids[:, None] == jnp.arange(lengths.shape[0], dtype=jnp.int32)[None, :]).astype(jnp.int32)
    doc_begin = jnp.sum(onehot * starts[None, :], axis=1)
    tenant = jnp.sum(onehot * tenants[None, :], axis=1)
    head_len = jnp.sum(onehot * prompt_len[None, :], axis=1)
    within = token_pos - doc_begin
    return doc_begin, within, tenant, within < head_len


def body(hidden_in, prompt_table, norm_gain, w_qkv, w_out, doc_lengths, doc_tenant, prompt_lengths):
    s = lax.axis_index("seq")
    token_pos = s * POS + jnp.arange(POS, dtype=jnp.int32)
    table = jax.vmap(doc_table, in_axes=(0, 0, 0, None))
    begin, within, tenant, prompt = table(doc_lengths, doc_tenant, prompt_lengths, token_pos)
    flat_table = prompt_table.reshape(TENANTS * PLEN, FEAT)
    table_slot = tenant * PLEN + jnp.minimum(within, PLEN - 1)
    picker = (table_slot[..., None] == jnp.arange(TENANTS * PLEN, dtype=jnp.int32)).astype(BF16)
    lookup = jnp.einsum("rsk,kd->rsd", picker, flat_table, preferred_element_type=F32).astype(BF16)
    embedded = jnp.where(prompt[..., None], lookup, hidden_in)
    packed = [jnp.concatenate([embedded[r, :HALF], embedded[r, HALF:]], axis=1) for r in range(2)]

    half_dim = HEAD_DIM // 2
    inverse_freq = THETA ** (-jnp.arange(half_dim, dtype=F32) / half_dim)
    angles = within.astype(F32)[..., None] * inverse_freq
    cosine, sine = jnp.cos(angles), jnp.sin(angles)
    cos = jnp.concatenate([cosine, cosine], axis=2)
    sin = jnp.concatenate([-sine, sine], axis=2)
    gain = norm_gain.reshape(RING, 1, FEAT)
    owner = jnp.where(prompt, -1, tenant)[..., None]
    begin_col = begin[..., None]

    w_mine = jnp.pad(w_out, ((0, SLOT - SHARD), (0, 0))).reshape(SLOT, RING, FEAT)
    w_all = lax.all_gather(jnp.transpose(w_mine, (1, 0, 2)), "seq", axis=0)
    rows = np.arange(GROUP * HEAD_DIM)
    perm = np.zeros((GROUP * HEAD_DIM, DEPTH), np.float32)
    perm[rows, rows // SHARD * SLOT + rows % SHARD] = 1
    perm = jnp.asarray(perm, BF16)

    project_flops = 2 * POS * D * COLS
    q0, kv0 = call(
        project_kernel, 1, (Q_SHAPE, KV_SHAPE), [VM, VM, ANY, VM, VM], (VM, VM), FEATURE_SCRATCH, 40, project_flops
    )(packed[0], gain, w_qkv, cos[0], sin[0])
    q1, kv1, keys0 = call(
        project_keys_kernel, 2, (Q_SHAPE, KV_SHAPE, KEYS_SHAPE), [VM, VM, ANY, VM, VM, VM], (VM, VM, ANY),
        FEATURE_SCRATCH + KEY_SCRATCH, 40, project_flops,
    )(packed[1], gain, w_qkv, cos[1], sin[1], kv0)
    keys1 = call(keys_kernel, 3, KEYS_SHAPE, [VM], ANY, KEY_SCRATCH, 16, 2**20)(kv1)

    count = (s - begin[:, 0] // POS) // 2 + 1
    smem = pl.BlockSpec(memory_space=pltpu.SMEM)
    ctx0, ctx1 = call(
        attend_kernel, None, (CTX_SHAPE, CTX_SHAPE), [smem] + [VM] * 6, (VM, VM), ATTEND_SCRATCH, 48,
        8 * project_flops,
    )(count, q0, q1, keys0, keys1, begin_col[0], begin_col[1])

    out0, loss0 = call(
        sums_kernel, 4, (OUT_SHAPE, LOSS_SHAPE), [VM, VM, ANY, VM, VM], (VM, VM), SUM_SCRATCH, 40, project_flops
    )(ctx0, perm, w_all, packed[0], owner[0])
    loss_scratch = [
        pltpu.VMEM((3, RING, 8, HEAD_DIM), F32),
        pltpu.SemaphoreType.DMA((3, RING)),
        pltpu.SemaphoreType.DMA((3, RING)),
    ]
    out1, loss = call(
        last_kernel, 5, (OUT_SHAPE, LOSS_SHAPE), [VM, VM, ANY, VM, VM, VM], (VM, VM),
        SUM_SCRATCH + loss_scratch, 40, project_flops,
    )(ctx1, perm, w_all, packed[1], owner[1], loss0)
    return jnp.stack([out0, out1]), loss[0, :TENANTS]


def solution(mesh):
    placed = (
        P(None, "seq", "tensor"),
        P(None, None, "tensor"),
        P(),
        P(None, "tensor"),
        P(("tensor", "seq"), None),
        P(),
        P(),
        P(),
    )
    return jax.shard_map(
        body, mesh=mesh, in_specs=placed, out_specs=(P(None, "seq", "tensor"), P()), check_vma=False
    )
```

time: 600 us -> 225 us (0.38)
  matrix products: 223 us -> 0.48 us
  waiting for transfers between devices: 205 us -> 0.02 us
  Pallas kernels: 0 us -> 182 us
  blocking collectives: 76.4 us -> 0 us
  other arithmetic: 69.8 us -> 3.89 us
  local copies, waits for them, and re-layouts: 9.23 us -> 23.7 us
    dot_general x35 -> x1, matrix products: 223 us -> 0.48 us  [body(): jnp.einsum('rsk,kd->rsd', picker, flat_table, preferred_element_type=F32)]
    pallas_call x0 -> x6, Pallas kernels: none -> 182 us  [the longest x1 59.1 us: body(): call(last_kernel, 5, (OUT_SHAPE, LOSS_SHAPE), [VM, VM, ANY, VM, VM, VM],...]
    all_gather x3 -> x1, waiting for transfers between devices: 154 us -> 0.01 us  [body(): w_all = lax.all_gather(jnp.transpose(w_mine, (1, 0, 2)), 'seq', axis=0)]
    psum x1 -> x0, blocking collectives: 76.4 us -> none  [body(): lax.psum(jnp.sum(owner * proxy[..., None], axis=(0, 1)), ('seq', 'tensor'))]
    reduce_scatter x1 -> x0, waiting for transfers between devices: 49.9 us -> none  [body(): lax.psum_scatter(partial_value.astype(jnp.bfloat16), 'tensor', scatter_di...]
    reduce_sum x19 -> x0, other arithmetic: 34.4 us -> none  [the longest x16 29.5 us: one_block(): totals = totals * rescale + jnp.sum(weights, axis=4)]
    add x34 -> x2, other arithmetic: 20.7 us -> 0.02 us  [the longest x1 0.02 us: body(): count = (s - begin[:, 0] // POS) // 2 + 1]
    unnamed x7 -> x24, local copies, waits for them, and re-layouts: 8.48 us -> 18.3 us
  transfers between devices with their start and end apart: 4 -> 1, of which waited for: 4 -> 0; matrix products, arithmetic and copies ran while one was open for 4% -> 4% of each run, Pallas kernels for 0% -> 44%
where the time goes in v1:
time: 225 us; the launch traced here: 224 us
  Pallas kernels  182 us (81%)
  local copies, waits for them, and re-layouts  23.7 us (11%)
  between operations  14.3 us (6%)
  other arithmetic  3.89 us (2%)
    pallas_call x1, Pallas kernels, body(): call(last_kernel, 5, (OUT_SHAPE, LOSS_SHAPE), [VM, VM, ANY, VM, VM, VM],...  59.1 us
    pallas_call x1, Pallas kernels, body(): call(project_keys_kernel, 2, (Q_SHAPE, KV_SHAPE, KEYS_SHAPE), [VM, VM, AN...  35.8 us
    pallas_call x1, Pallas kernels, body(): call(project_kernel, 1, (Q_SHAPE, KV_SHAPE), [VM, VM, ANY, VM, VM], (VM,...  29.3 us
    pallas_call x1, Pallas kernels, body(): call(sums_kernel, 4, (OUT_SHAPE, LOSS_SHAPE), [VM, VM, ANY, VM, VM], (VM,...  25 us
    pallas_call x1, Pallas kernels, body(): call(keys_kernel, 3, KEYS_SHAPE, [VM], ANY, KEY_SCRATCH, 16, 2 ** 20)(kv1)  24.8 us
    unnamed x24, local copies, waits for them, and re-layouts  18.3 us
    pallas_call x1, Pallas kernels, body(): call(attend_kernel, None, (CTX_SHAPE, CTX_SHAPE), [smem] + [VM] * 6, (VM,...  7.8 us
  transfers between devices with their start and end apart: 1, of which 0 were waited for; matrix products, arithmetic and copies ran while one was open for 4% of the time, Pallas kernels for 44%

profile of v1, /device:TPU:1, one launch (start us, length us, event | category | flops | bytes accessed | tf_op | source)
XLA Modules:
  0.0 224.2 jit_solution(6022769908974544346)
XLA Ops:
  7.2 1.0 pad.4
  8.2 0.3 reshape.95
  8.6 0.8 copy.47
  9.4 0.9 reduce_window_sum.11
  10.2 0.7 sub.39
  10.9 1.2 copy.44
  12.1 0.8 reshape.94.gain
  13.1 0.8 select_reduce_fusion.1
  13.9 0.8 copy.45.begin0
  14.7 0.8 copy.46.begin1
  15.5 0.1 copy.48.owner
  15.6 0.1 copy.49.owner
  15.8 0.5 fusion
  16.3 0.1 pad_maximum_fusion.1
  16.5 1.0 multiply_sine_fusion
  17.5 0.2 fusion.6
  17.7 3.3 %copy-done.2 = bf16[3584,1152]{1,0:T(8,128)(2,1)S(1)} copy-done((bf16[3584,1152]{1,0:T(8,128)(2,1)S(1)}, bf16[3584,1152]{1,0:T(8,128)(2,1)}, u32[]{:S(2)}) %copy-start.2) | copy-done | bytes 8257560
  21.0 29.3 %project_kernel.1 = (bf16[7,256,128]{2,1,0:T(8,128)(2,1)S(1)}, bf16[256,256]{1,0:T(8,128)(2,1)S(1)}) custom-call(bf16[128,896]{1,0:T(8,128)(2,1)S(1)} %get-tuple-element.56.x.emb, f32[8,1,448]{2,1,0:T(1,128)S(1)} %reshape.94.gain, bf16[3584,1152]{1,0:T(8,128)(2,1)S(1)} %copy-done.2, f32[256,128]{1,0:T(8,128)S(1)} %get-tuple-element.58.cos, ...), custom_call_target="tpu_custom_call" | custom-call | flops 2113929216 | bytes 8388608 | tf_op jit(solution)/shard_map/project_kernel/pallas_call | solution.py:552
  50.3 3.7 %copy-done.3 = bf16[3584,1152]{1,0:T(8,128)(2,1)S(1)} copy-done((bf16[3584,1152]{1,0:T(8,128)(2,1)S(1)}, bf16[3584,1152]{1,0:T(8,128)(2,1)}, u32[]{:S(2)}) %copy-start.3) | copy-done | bytes 8257560
  54.0 35.8 %project_keys_kernel.1 = (bf16[7,256,128]{2,1,0:T(8,128)(2,1)S(1)}, bf16[256,256]{1,0:T(8,128)(2,1)S(1)}, bf16[32,256,256]{2,1,0:T(8,128)(2,1)S(1)}) custom-call(bf16[128,896]{1,0:T(8,128)(2,1)S(1)} %get-tuple-element.57.x.emb, f32[8,1,448]{2,1,0:T(1,128)S(1)} %reshape.94.gain, bf16[3584,1152]{1,0:T(8,128)(2,1)S(1)} %copy-done.3, ...), custom_call_target="tpu_custom_call" | custom-call | flops 2113929216 | bytes 8388608 | tf_op jit(solution)/shard_map/project_keys_kernel/pallas_call | solution.py:555
  89.8 2.0 copy-done.10
  91.8 24.8 %keys_kernel.1.kv1 = bf16[32,256,256]{2,1,0:T(8,128)(2,1)S(1)} custom-call(bf16[256,256]{1,0:T(8,128)(2,1)S(1)} %get-tuple-element.17.own), custom_call_target="tpu_custom_call" | custom-call | flops 1048576 | bytes 8388608 | tf_op jit(solution)/shard_map/keys_kernel/pallas_call | solution.py:559
  116.6 1.9 copy-done.5
  118.5 0.1 slice_reduce_fusion
  118.7 7.8 %attend_kernel.1 = (bf16[256,896]{1,0:T(8,128)(2,1)S(1)}, bf16[256,896]{1,0:T(8,128)(2,1)S(1)}) custom-call(s32[2]{0:T(128)S(1)} %fusion.9.count, bf16[7,256,128]{2,1,0:T(8,128)(2,1)S(1)} %get-tuple-element.13.q0, bf16[7,256,128]{2,1,0:T(8,128)(2,1)S(1)} %get-tuple-element.15.q1, bf16[32,256,256]{2,1,0:T(8,128)(2,1)} %copy-done.10, ...), custom_call_target="tpu_custom_call" | custom-call | flops 16911433728 | bytes 8388608 | tf_op jit(solution)/shard_map/attend_kernel/pallas_call | solution.py:563
  126.5 0.8 copy-done.6
  127.3 3.4 %copy-done.1 = bf16[256,32,448]{2,1,0:T(8,128)(2,1)S(1)} copy-done((bf16[256,32,448]{2,1,0:T(8,128)(2,1)S(1)}, bf16[256,32,448]{2,1,0:T(8,128)(2,1)}, u32[]{:S(2)}) %copy-start.1) | copy-done | bytes 7340056
  130.7 1.0 copy-done.7
  131.7 25.0 %sums_kernel.1 = (bf16[256,448]{1,0:T(8,128)(2,1)S(1)}, f32[8,128]{1,0:T(8,128)S(1)}) custom-call(bf16[256,896]{1,0:T(8,128)(2,1)S(1)} %copy-done.7, bf16[896,1024]{1,0:T(8,128)(2,1)S(1)} %copy-done.4, bf16[32,8,32,448]{3,2,1,0:T(8,128)(2,1)S(1)} %bitcast.35, bf16[128,896]{1,0:T(8,128)(2,1)S(1)} %get-tuple-element.56.x.emb, s32[256,1]{1,0:T(8,128)S(1)} %copy.48.owner), custom_call_target="tpu_custom_call" | custom-call | flops 2113929216 | bytes 8388608 | tf_op jit(solution)/shard_map/sums_kernel/pallas_call | solution.py:568
  156.7 59.1 %last_kernel.1 = (bf16[256,448]{1,0:T(8,128)(2,1)S(1)}, f32[8,128]{1,0:T(8,128)S(1)}) custom-call(bf16[256,896]{1,0:T(8,128)(2,1)S(1)} %get-tuple-element.20.ctx, bf16[896,1024]{1,0:T(8,128)(2,1)S(1)} %copy-done.4, bf16[32,8,32,448]{3,2,1,0:T(8,128)(2,1)S(1)} %bitcast.36, bf16[128,896]{1,0:T(8,128)(2,1)S(1)} %get-tuple-element.57.x.emb, ...), custom_call_target="tpu_custom_call" | custom-call | flops 2113929216 | bytes 8388608 | tf_op jit(solution)/shard_map/last_kernel/pallas_call | solution.py:576
  215.9 1.0 copy.50
  216.9 0.5 slice_bitcast_fusion.8
  (28 shorter events, 0.3 us)
Async XLA Ops:
  7.2 8.6 %copy-start = (bf16[16,32,448]{2,1,0:T(8,128)(2,1)S(1)}, bf16[16,32,448]{2,1,0:T(8,128)(2,1)}, u32[]{:S(2)}) copy-start(bf16[16,32,448]{2,1,0:T(8,128)(2,1)} %param.10) | copy-start | bytes 1376260
  7.2 120.1 %all-gather.3.cloned.1.call-start = ((), (), s32[]{:S(2)}) async-start(), calls=%async_computation | async-start | bytes 8650752 | tf_op jit(solution)/shard_map/all_gather | solution.py:545
  17.7 3.3 %copy-start.2 = (bf16[3584,1152]{1,0:T(8,128)(2,1)S(1)}, bf16[3584,1152]{1,0:T(8,128)(2,1)}, u32[]{:S(2)}) copy-start(bf16[3584,1152]{1,0:T(8,128)(2,1)} %w.3) | copy-start | bytes 24772612
  50.3 3.7 %copy-start.3 = (bf16[3584,1152]{1,0:T(8,128)(2,1)S(1)}, bf16[3584,1152]{1,0:T(8,128)(2,1)}, u32[]{:S(2)}) copy-start(bf16[3584,1152]{1,0:T(8,128)(2,1)} %w.3) | copy-start | bytes 24772612
  89.8 2.0 copy-start.10
  91.8 26.9 %copy-start.8 = (s32[256,1]{1,0:T(8,128)S(1)}, s32[256,1]{1,0:T(8,128)}, u32[]{:S(2)}) copy-start(s32[256,1]{1,0:T(8,128)} %copy.45.begin0) | copy-start | bytes 3076
  91.8 26.9 %copy-start.9 = (s32[256,1]{1,0:T(8,128)S(1)}, s32[256,1]{1,0:T(8,128)}, u32[]{:S(2)}) copy-start(s32[256,1]{1,0:T(8,128)} %copy.46.begin1) | copy-start | bytes 3076
  116.6 1.9 copy-start.5
  118.7 8.6 %copy-start.4 = (bf16[896,1024]{1,0:T(8,128)(2,1)S(1)}, bf16[896,1024]{1,0:T(8,128)(2,1)}, u32[]{:S(2)}) copy-start(bf16[896,1024]{1,0:T(8,128)(2,1)} %constant.56.clone.perm) | copy-start | bytes 5505028
  126.5 0.8 copy-start.6
  127.3 3.4 %copy-start.1 = (bf16[256,32,448]{2,1,0:T(8,128)(2,1)S(1)}, bf16[256,32,448]{2,1,0:T(8,128)(2,1)}, u32[]{:S(2)}) copy-start(bf16[256,32,448]{2,1,0:T(8,128)(2,1)} %all-gather.3.cloned.1.call-done) | copy-start | bytes 22020100
  130.7 1.0 copy-start.7
Sparse Core Ops, SparseCore 0:
  10.6 65.6 all-gather.2

commit v2 on v0

v2 whole, which is shorter than its diff:
```python
import jax
import jax.numpy as jnp
import numpy as np
from jax import lax
from jax.experimental import pallas as pl
from jax.experimental.pallas import tpu as pltpu
from jax.sharding import PartitionSpec as P

D = 3584
HEAD_DIM = 128
GROUP = 7
TENANTS = 16
PLEN = 32
THETA = 5000000.0
EPS = 1e-05

DOCS = 16
SEQ = 32
RING = 8
POS = 256
FEAT = 448
HALF = POS // 2
WIDE = 2 * FEAT
SUB = HALF // 2
COLS = (GROUP + 2) * HEAD_DIM
SHARD = 28
SLOT = 32
DEPTH = SEQ * SLOT
WINDOW = 9
QSCALE = HEAD_DIM**-0.5 * 1.4426950408889634
LOW = -1e30
MESH = pl.DeviceIdType.MESH
F32 = jnp.float32
BF16 = jnp.bfloat16


def dot(a, b):
    return jnp.dot(a, b, preferred_element_type=F32)


def place():
    return lax.axis_index("seq"), lax.axis_index("tensor")


def ring_peers():
    s, z = place()
    return [(s, lax.rem(z + 1, RING)), (s, lax.rem(z + RING - 1, RING))]


def push(src, dst, send, recv, peer):
    return pltpu.make_async_remote_copy(
        src_ref=src, dst_ref=dst, send_sem=send, recv_sem=recv, device_id=peer, device_id_type=MESH
    )


def unpack(x):
    return jnp.concatenate([x[:, :FEAT], x[:, FEAT:]], axis=0)


def pack(x):
    return jnp.concatenate([x[:HALF], x[HALF:]], axis=1)


class Ring:
    def __init__(self, x, buf, send, recv):
        self.x, self.buf, self.send, self.recv = x, buf, send, recv
        self.z = place()[1]
        self.peers = ring_peers()

    def piece(self, way, hop, sub, mine):
        step = 1 if way == 0 else RING - 1
        origin = lax.rem(self.z + (RING - step) * (hop - 1 if mine else hop), RING)
        rows = pl.ds(sub * SUB, SUB)
        src = self.x.at[rows] if mine and hop == 1 else self.buf.at[origin, rows]
        index = (way, hop - 1, sub)
        return push(src, self.buf.at[origin, rows], self.send.at[index], self.recv.at[index], self.peers[way])

    def start(self):
        for sub in range(2):
            for way in range(2):
                self.piece(way, 1, sub, True).start()

    def relay(self, hop, sub):
        for way in range(2):
            if hop < 4 or sub == way:
                self.piece(way, hop, sub, False).wait_recv()
            if hop < 3 or (hop == 3 and sub == way):
                self.piece(way, hop + 1, sub, True).start()

    def block(self, away):
        origin = lax.rem(self.z + away, RING)
        return self.buf[origin], origin

    def drain(self):
        for hop in range(1, 5):
            for sub in range(2):
                for way in range(2):
                    if hop < 4 or sub == way:
                        self.piece(way, hop, sub, True).wait_send()


class Projection:
    def __init__(self, gain, w, wbuf, wsem, acc, ssq):
        self.gain, self.w = gain, w
        self.wbuf, self.wsem, self.acc, self.ssq = wbuf, wsem, acc, ssq

    def fetch(self):
        z = place()[1]
        for away in (0, 7, 1, 6, 2, 5, 3, 4):
            self.copy(lax.rem(z + away, RING)).start()

    def copy(self, origin):
        return pltpu.make_async_copy(
            self.w.at[pl.ds(origin * FEAT, FEAT)], self.wbuf.at[origin], self.wsem.at[origin]
        )

    def absorb(self, x, origin, fresh, first):
        if fresh:
            self.copy(origin).wait()
        wide = unpack(x).astype(F32)
        square = jnp.sum(wide * wide, axis=1, keepdims=True)
        scaled = (wide * self.gain[origin]).astype(BF16)
        product = dot(scaled, self.wbuf[origin])
        if first:
            self.ssq[...] = jnp.broadcast_to(square, self.ssq.shape)
            self.acc[...] = product
        else:
            self.ssq[...] += square
            self.acc[...] += product

    def finish(self, cos, sin, q, kv):
        scale = lax.rsqrt(self.ssq[...] / D + EPS)

        def rotated(n):
            part = self.acc[:, n * HEAD_DIM : (n + 1) * HEAD_DIM] * scale
            return part * cos[...] + pltpu.roll(part, HEAD_DIM // 2, 1) * sin[...]

        kv[:HEAD_DIM] = rotated(GROUP).T.astype(BF16)
        value = (self.acc[:, (GROUP + 1) * HEAD_DIM :] * scale).astype(BF16)
        kv[HEAD_DIM:] = pack(value)

        def queries():
            for n in range(GROUP):
                q[n] = (rotated(n) * QSCALE).astype(BF16)

        return queries


def plane_peers():
    s, z = place()
    x, y, c = s // 8, lax.rem(s // 2, 4), lax.rem(s, 2)

    def at(a, b):
        dx, dy = a * (1 - c) + b * c, a * c + b * (1 - c)
        return lax.rem(x + dx, 4) * 8 + lax.rem(y + dy, 4) * 2 + c

    return at, [(at(1, 0), z), (at(3, 0), z)], [(at(0, 1), z), (at(0, 3), z)], (s + 1 - 2 * c, z)


BACK = (3, 1)
KEY_SEMS = 36


class Plane:
    def __init__(self, own, everyone, send, recv, local):
        self.own, self.everyone, self.send, self.recv, self.local = own, everyone, send, recv, local
        at, self.first, self.second, self.sibling = plane_peers()
        self.s = place()[0]
        self.slots = {(a, b): at(a, b) for a in range(4) for b in range(4)}
        c = lax.rem(self.s, 2)
        x, y = self.s // 8, lax.rem(self.s // 2, 4)
        self.theirs = {}
        for a in range(4):
            for b in range(4):
                dx, dy = a * c + b * (1 - c), a * (1 - c) + b * c
                self.theirs[a, b] = lax.rem(x + dx, 4) * 8 + lax.rem(y + dy, 4) * 2 + 1 - c
        half = own.shape[0] // 2
        self.halves = (pl.ds(0, half), pl.ds(half, half))
        self.sent = {}

    def move(self, key, slot=None):
        kind, a, b, way = key
        rows = None
        if kind == "p1":
            index, peer = way, self.first[way]
        elif kind == "p2":
            index, peer, rows = 2 + way, self.first[way], self.halves[way]
        elif kind == "s1":
            index, peer = 4 + 4 * a + way, self.second[way]
        elif kind == "s2":
            index, peer, rows = 6 + 4 * a + way, self.second[way], self.halves[way]
        else:
            index, peer = 20 + 4 * a + b, self.sibling
        if slot is None:
            slot = self.slots[a, b]
        ref = self.everyone.at[slot, rows] if rows is not None else self.everyone.at[slot]
        src = self.own if (a, b) == (0, 0) and rows is None else ref
        return push(src, ref, self.send.at[index], self.recv.at[index], peer)

    def go(self, *key):
        self.sent[key] = True
        self.move(key).start()

    def await_(self, slot, *key):
        self.move(key, slot).wait_recv()

    def keep(self):
        return pltpu.make_async_copy(self.own, self.everyone.at[self.s], self.local)

    def start(self):
        self.keep().start()
        for way in range(2):
            self.go("p1", 0, 0, way)
        self.spread(0)

    def spread(self, a):
        for way in range(2):
            self.go("s1", a, 0, way)
        self.go("sib", a, 0, 0)

    def first_hop(self):
        for way in range(2):
            a = BACK[way]
            self.await_(self.slots[a, 0], "p1", 0, 0, way)
            self.go("p2", a, 0, way)
            self.spread(a)

    def second_hop(self):
        for way in range(2):
            self.await_(self.slots[2, 0], "p2", BACK[way], 0, way)
        self.spread(2)

    def cross(self, a):
        for way in range(2):
            b = BACK[way]
            self.await_(self.slots[a, b], "s1", a, 0, way)
            self.go("s2", a, b, way)
            self.go("sib", a, b, 0)

    def far(self, a):
        for way in range(2):
            self.await_(self.slots[a, 2], "s2", a, BACK[way], way)
        self.go("sib", a, 2, 0)

    def finish(self):
        for a in range(4):
            for b in range(4):
                self.await_(self.theirs[a, b], "sib", a, b, 0)
        self.keep().wait()

    def drain(self):
        for key in self.sent:
            self.move(key).wait_send()

    def steps(self):
        cross, far = self.cross, self.far
        return [
            self.first_hop, lambda: cross(0), self.second_hop, lambda: cross(3), lambda: cross(1),
            lambda: far(0), lambda: cross(2), lambda: far(3), lambda: far(1), lambda: far(2),
        ]


def attend(step, q, kv, begin, acc, top):
    s, _ = place()
    last = s - 2 * step
    low = jnp.maximum(last - 1, 0)
    key_pos = low * POS + lax.broadcasted_iota(jnp.int32, (POS, 2 * POS), 1)
    query_pos = s * POS + lax.broadcasted_iota(jnp.int32, (POS, 2 * POS), 0)
    allowed = (key_pos >= jnp.concatenate([begin] * 4, axis=1)) & (key_pos <= jnp.minimum(query_pos, last * POS + POS - 1))
    bias = jnp.where(allowed, 0.0, LOW)
    blocks = kv[pl.ds(low, 2)]
    keys = jnp.concatenate([blocks[0, :HEAD_DIM], blocks[1, :HEAD_DIM]], axis=1)
    values = [blocks[n, HEAD_DIM:, m * HEAD_DIM : (m + 1) * HEAD_DIM] for n in (0, 1) for m in (0, 1)]
    values = jnp.concatenate(values, axis=0)
    values = jnp.concatenate([values, jnp.ones_like(values)], axis=1)
    for n in range(GROUP):
        scores = dot(q[n], keys) + bias
        old = top[n]
        new = jnp.maximum(old, jnp.max(scores, axis=1, keepdims=True))
        weights = jnp.exp2(scores - jnp.concatenate([new] * 4, axis=1)).astype(BF16)
        rescale = jnp.exp2(old - new)
        acc[n] = acc[n] * jnp.concatenate([rescale] * 2, axis=1) + dot(weights, values)
        top[n] = new


def finish_attend(acc, ctx):
    for n in range(GROUP):
        both = acc[n]
        ctx[:, n * HEAD_DIM : (n + 1) * HEAD_DIM] = (both[:, :HEAD_DIM] / both[:, HEAD_DIM:]).astype(BF16)


class Sums:
    def __init__(self, wall, ctx, parts, out, came, send, recv):
        self.wall, self.ctx, self.parts = wall, ctx, parts
        self.out, self.came, self.send, self.recv = out, came, send, recv
        self.peers = ring_peers()
        self.z = place()[1]

    def part(self, away):
        owner = lax.rem(self.z + away, RING)
        odd = lax.rem(owner, 2)
        begin = pl.multiple_of(owner // 2 * WIDE + odd * (FEAT - 64), 128)
        w = self.wall[:, :, pl.ds(begin, 512)].reshape(DEPTH, 512)
        product = dot(self.ctx[...], w)
        product = jnp.where(odd == 1, product[:, 64:], product[:, :FEAT])
        return pack(product)

    def move(self, way, k, sub):
        rows = pl.ds(sub * SUB, SUB)
        index = (way, k, sub)
        return push(
            self.out.at[way, k, rows], self.came.at[way, k, rows],
            self.send.at[index], self.recv.at[index], self.peers[way],
        )

    def ship(self, way, k, sub, value):
        self.out[way, k, pl.ds(sub * SUB, SUB)] = value.astype(BF16)
        self.move(way, k, sub).start()

    def arrived(self, way, k, sub):
        self.move(way, k, sub).wait_recv()
        return self.came[way, k, pl.ds(sub * SUB, SUB)].astype(F32)

    def first(self):
        value = self.part(4)
        for way in range(2):
            self.ship(way, 0, way, value[way * SUB : (way + 1) * SUB])

    def ready(self, k):
        self.parts[0] = self.part(4 - k)
        self.parts[1] = self.part(4 + k)

    def turn(self, k, turn):
        for way in range(2):
            sub = 1 - (turn ^ way) if k == 1 else turn
            piece = self.parts[way, pl.ds(sub * SUB, SUB)]
            if k > 1 or sub == way:
                piece = piece + self.arrived(way, k - 1, sub)
            self.ship(way, k, sub, piece)

    def finish(self):
        self.parts[0] = self.part(0)
        for sub in range(2):
            rows = pl.ds(sub * SUB, SUB)
            self.parts[0, rows] = self.parts[0, rows] + self.arrived(0, 3, sub) + self.arrived(1, 3, sub)

    def drain(self):
        for way in range(2):
            for k in range(4):
                for sub in range(2):
                    if k > 0 or sub == way:
                        self.move(way, k, sub).wait_send()

    def steps(self):
        def both(k):
            self.ready(k)
            self.turn(k, 0)

        return [
            self.first,
            lambda: both(1), lambda: self.turn(1, 1),
            lambda: both(2), lambda: self.turn(2, 1),
            lambda: both(3), lambda: self.turn(3, 1),
        ]


def emit(delta, x, owner, out):
    delta = unpack(delta)
    out[...] = (unpack(x).astype(F32) + delta).astype(BF16)
    proxy = jnp.sum(delta * delta, axis=1, keepdims=True) / D
    lanes = lax.broadcasted_iota(jnp.int32, (POS, HEAD_DIM), 1)
    total = jnp.sum(jnp.where(owner[...] == lanes, proxy, 0.0), axis=0, keepdims=True)
    return jnp.broadcast_to(total, (8, HEAD_DIM))


def loss_groups():
    s, z = place()
    x, y, c = s // 8, lax.rem(s // 2, 4), lax.rem(s, 2)
    xc = x * 2 + c
    return [
        (z, 8, lambda n: (s, n)),
        (xc, 8, lambda n: ((n // 2) * 8 + y * 2 + lax.rem(n, 2), z)),
        (y, 4, lambda n: (x * 8 + n * 2 + c, z)),
    ]


def loss_peers():
    return [who(lax.rem(me + j, n)) for me, n, who in loss_groups() for j in range(1, n)]


def loss_total(value, slots, send, recv):
    for stage, (me, n, who) in enumerate(loss_groups()):
        slots[stage, me] = value
        sent = []
        for j in range(1, n):
            ref = slots.at[stage, me]
            copy = push(ref, ref, send.at[stage, j], recv.at[stage, j], who(lax.rem(me + j, n)))
            copy.start()
            sent.append(copy)
        for j in range(1, n):
            ref = slots.at[stage, lax.rem(me + n - j, n)]
            push(ref, ref, send.at[stage, j], recv.at[stage, j], who(lax.rem(me + j, n))).wait_recv()
        value = slots[stage, 0]
        for j in range(1, n):
            value = value + slots[stage, j]
        for copy in sent:
            copy.wait_send()
    return value


def describe(row, lengths, tenants, prompts):
    pos = place()[0] * POS + lax.broadcasted_iota(jnp.int32, (POS, HEAD_DIM), 0)
    begin = jnp.zeros_like(pos)
    tenant = jnp.full_like(pos, tenants[row, 0])
    prompt = jnp.full_like(pos, prompts[row, 0])
    start = jnp.int32(0)
    for doc in range(1, DOCS):
        start = start + lengths[row, doc - 1]
        inside = pos >= start
        begin = jnp.where(inside, start, begin)
        tenant = jnp.where(inside, tenants[row, doc], tenant)
        prompt = jnp.where(inside, prompts[row, doc], prompt)
    return begin, pos - begin, tenant, prompt


def embed(row, hidden, table, lengths, tenants, prompts, x, begin_ref, within_ref, owner_ref):
    begin, within, tenant, prompt = describe(row, lengths, tenants, prompts)
    begin_ref[row] = begin
    within_ref[row] = within
    owner_ref[row] = jnp.where(within < prompt, -1, tenant)
    slot = tenant * PLEN + jnp.minimum(within, PLEN - 1)
    entries = lax.broadcasted_iota(jnp.int32, (POS, TENANTS * PLEN), 1)
    picker = jnp.where(jnp.concatenate([slot] * 4, axis=1) == entries, 1.0, 0.0).astype(BF16)
    lookup = dot(picker, table[...])
    left = jnp.concatenate([prompt - within] * 4, axis=1)[:, :FEAT]
    x[row] = pack(jnp.where(left > 0, lookup, hidden[row].astype(F32)).astype(BF16))


def block_kernel(
    hidden, table, gain, w, w_out, lengths, tenants, prompts, freq, perm,
    out, loss,
    x, begin, within, owner, cos, sin, gains,
    wbuf, wsem, acc, ssq, buf0, buf1, fsend0, frecv0, fsend1, frecv1,
    q, own, keys0, keys1, ksend0, krecv0, ksend1, krecv1, klocal,
    wpad, wall, osend, orecv, olocal, permbuf, psem,
    total, top, ctx, mixed, parts,
    sout0, came0, ssend0, srecv0, sout1, came1, ssend1, srecv1,
    slots, lsend, lrecv,
):
    s, _ = place()
    peers = loss_peers()
    barrier = pltpu.get_barrier_semaphore()
    for peer in peers:
        pl.semaphore_signal(barrier, inc=1, device_id=peer, device_id_type=MESH)
    proj = Projection(gains, w, wbuf, wsem, acc, ssq)
    proj.fetch()
    perm_copy = pltpu.make_async_copy(perm, permbuf, psem)
    perm_copy.start()
    doc_refs = (lengths, tenants, prompts)
    embed(0, hidden, table, *doc_refs, x, begin, within, owner)
    wpad[:SHARD] = w_out[...]
    wpad[SHARD:] = jnp.zeros((SLOT - SHARD, D), BF16)
    for n in range(RING):
        gains[n] = gain[:, n * FEAT : (n + 1) * FEAT]
    pl.semaphore_wait(barrier, len(peers))

    ring = [Ring(x.at[0], buf0, fsend0, frecv0), Ring(x.at[1], buf1, fsend1, frecv1)]
    weights = Plane(wpad, wall, osend, orecv, olocal)
    keys = [
        Plane(own.at[0], keys0, ksend0, krecv0, klocal.at[0]),
        Plane(own.at[1], keys1, ksend1, krecv1, klocal.at[1]),
    ]
    sums = [
        Sums(wall, mixed, parts, sout0, came0, ssend0, srecv0),
        Sums(wall, mixed, parts, sout1, came1, ssend1, srecv1),
    ]

    def angles(row):
        angle = within[row].astype(F32) * freq[...]
        lane = lax.broadcasted_iota(jnp.int32, (POS, HEAD_DIM), 1)
        cos[row] = jnp.cos(angle)
        sine = jnp.sin(angle)
        sin[row] = jnp.where(lane < HEAD_DIM // 2, -sine, sine)

    def gather(row, between):
        between = list(between)

        def other(n=1):
            for _ in range(n):
                if between:
                    between.pop(0)()

        proj.absorb(x[row], place()[1], row == 0, True)
        other()
        for hop in range(1, 4):
            ring[row].relay(hop, 0)
            other()
            ring[row].relay(hop, 1)
            other()
            if hop == 3 and row == 0:
                ring[1].start()
            proj.absorb(*ring[row].block(RING - hop), row == 0, False)
            other()
            proj.absorb(*ring[row].block(hop), row == 0, False)
        for sub in range(2):
            ring[row].relay(4, sub)
        proj.absorb(*ring[row].block(4), row == 0, False)
        return between

    def queries_keys(row):
        queries = proj.finish(cos.at[row], sin.at[row], q.at[row], own.at[row])
        keys[row].start()
        queries()

    def attention(row, between):
        total[...] = jnp.zeros_like(total)
        top[...] = jnp.full_like(top, LOW)
        everyone = (keys0, keys1)[row]

        def step(n, carry):
            @pl.when(s >= 2 * n)
            def _():
                attend(n, q.at[row], everyone, begin[row], total, top)

            for at, one in enumerate(between):
                pl.when(n == at)(one)
            return carry

        lax.fori_loop(0, WINDOW, step, 0)
        finish_attend(total, ctx)

    ring[0].start()
    weights.start()
    embed(1, hidden, table, *doc_refs, x, begin, within, owner)
    angles(0)
    rest = gather(0, weights.steps()[:6] + [lambda: angles(1)])
    queries_keys(0)
    rest = rest + weights.steps()[6:]
    gather_steps = keys[0].steps()
    rest = gather(1, gather_steps[:6] + rest + gather_steps[6:])
    queries_keys(1)
    for one in rest:
        one()
    keys[0].finish()

    key_steps = keys[1].steps()
    attention(0, key_steps[:8] + [lambda: (key_steps[8](), key_steps[9]()) and None])
    weights.finish()
    keys[1].finish()
    perm_copy.wait()
    mixed[...] = dot(ctx[...], permbuf[...]).astype(BF16)
    attention(1, sums[0].steps())
    sums[0].finish()
    share = emit(parts[0], x[0], owner.at[0], out.at[0])
    mixed[...] = dot(ctx[...], permbuf[...]).astype(BF16)
    for one in sums[1].steps():
        one()
    sums[1].finish()
    share = share + emit(parts[0], x[1], owner.at[1], out.at[1])
    loss[...] = loss_total(share, slots, lsend, lrecv)
    for one in ring + [weights] + keys + sums:
        one.drain()


DMA = pltpu.SemaphoreType.DMA
RING_SEMS = DMA((2, 4, 2))
VM = pl.BlockSpec(memory_space=pltpu.VMEM)
SM = pl.BlockSpec(memory_space=pltpu.SMEM)
ANY = pl.BlockSpec(memory_space=pl.ANY)
SCRATCH = [
    pltpu.VMEM((2, HALF, WIDE), BF16),
    pltpu.VMEM((2, POS, HEAD_DIM), jnp.int32),
    pltpu.VMEM((2, POS, HEAD_DIM), jnp.int32),
    pltpu.VMEM((2, POS, HEAD_DIM), jnp.int32),
    pltpu.VMEM((2, POS, HEAD_DIM), F32),
    pltpu.VMEM((2, POS, HEAD_DIM), F32),
    pltpu.VMEM((RING, 1, FEAT), F32),
    pltpu.VMEM((RING, FEAT, COLS), BF16),
    DMA((RING,)),
    pltpu.VMEM((POS, COLS), F32),
    pltpu.VMEM((POS, HEAD_DIM), F32),
    pltpu.VMEM((RING, HALF, WIDE), BF16),
    pltpu.VMEM((RING, HALF, WIDE), BF16),
    RING_SEMS, RING_SEMS, RING_SEMS, RING_SEMS,
    pltpu.VMEM((2, GROUP, POS, HEAD_DIM), BF16),
    pltpu.VMEM((2, POS, 2 * HEAD_DIM), BF16),
    pltpu.VMEM((SEQ, POS, 2 * HEAD_DIM), BF16),
    pltpu.VMEM((SEQ, POS, 2 * HEAD_DIM), BF16),
    DMA((KEY_SEMS,)), DMA((KEY_SEMS,)), DMA((KEY_SEMS,)), DMA((KEY_SEMS,)),
    DMA((2,)),
    pltpu.VMEM((SLOT, D), BF16),
    pltpu.VMEM((SEQ, SLOT, D), BF16),
    DMA((KEY_SEMS,)), DMA((KEY_SEMS,)), DMA,
    pltpu.VMEM((GROUP * HEAD_DIM, DEPTH), BF16),
    DMA,
    pltpu.VMEM((GROUP, POS, 2 * HEAD_DIM), F32),
    pltpu.VMEM((GROUP, POS, HEAD_DIM), F32),
    pltpu.VMEM((POS, GROUP * HEAD_DIM), BF16),
    pltpu.VMEM((POS, DEPTH), BF16),
    pltpu.VMEM((2, HALF, WIDE), F32),
    pltpu.VMEM((2, 4, HALF, WIDE), BF16), pltpu.VMEM((2, 4, HALF, WIDE), BF16), RING_SEMS, RING_SEMS,
    pltpu.VMEM((2, 4, HALF, WIDE), BF16), pltpu.VMEM((2, 4, HALF, WIDE), BF16), RING_SEMS, RING_SEMS,
    pltpu.VMEM((3, RING, 8, HEAD_DIM), F32),
    DMA((3, RING)),
    DMA((3, RING)),
]


def body(hidden_in, prompt_table, norm_gain, w_qkv, w_out, doc_lengths, doc_tenant, prompt_lengths):
    freq = THETA ** (-np.arange(HEAD_DIM // 2) / (HEAD_DIM // 2))
    freq = jnp.asarray(np.concatenate([freq, freq])[None], F32)
    rows = np.arange(GROUP * HEAD_DIM)
    perm = np.zeros((GROUP * HEAD_DIM, DEPTH), np.float32)
    perm[rows, rows // SHARD * SLOT + rows % SHARD] = 1
    out, loss = pl.pallas_call(
        block_kernel,
        out_shape=(jax.ShapeDtypeStruct((2, POS, FEAT), BF16), jax.ShapeDtypeStruct((8, HEAD_DIM), F32)),
        in_specs=[VM, VM, VM, ANY, VM, SM, SM, SM, VM, ANY],
        out_specs=(VM, VM),
        scratch_shapes=SCRATCH,
        compiler_params=pltpu.CompilerParams(
            collective_id=1, has_side_effects=True, vmem_limit_bytes=60 * 2**20
        ),
        cost_estimate=pl.CostEstimate(flops=2 * 10**10, bytes_accessed=2 * 10**7, transcendentals=10**7),
        name="block",
    )(
        hidden_in, prompt_table.reshape(TENANTS * PLEN, FEAT), norm_gain[None], w_qkv, w_out,
        doc_lengths, doc_tenant, prompt_lengths, freq, jnp.asarray(perm, BF16),
    )
    return out, loss[0, :TENANTS]


def solution(mesh):
    placed = (
        P(None, "seq", "tensor"),
        P(None, None, "tensor"),
        P(),
        P(None, "tensor"),
        P(("tensor", "seq"), None),
        P(),
        P(),
        P(),
    )
    return jax.shard_map(
        body, mesh=mesh, in_specs=placed, out_specs=(P(None, "seq", "tensor"), P()), check_vma=False
    )
```

time: 600 us -> 157 us (0.26)
  matrix products: 223 us -> 0 us
  waiting for transfers between devices: 205 us -> 0 us
  Pallas kernels: 0 us -> 149 us
  blocking collectives: 76.4 us -> 0 us
  other arithmetic: 69.8 us -> 0 us
  between operations: 13.9 us -> 0.64 us
    dot_general x35 -> x0, matrix products: 223 us -> none  [the longest x16 116 us: one_block(): jnp.einsum('rgjsk,rkgh->rsgjh', weights.astype(jnp.bfloat16), block_kv[:,...]
    all_gather x3 -> x0, waiting for transfers between devices: 154 us -> none  [the longest x1 57.9 us: body(): pieces = lax.all_gather(key_value, 'seq', axis=1, tiled=True)]
    pallas_call x0 -> x1, Pallas kernels: none -> 149 us  [body(): pl.pallas_call(block_kernel, out_shape=(jax.ShapeDtypeStruct((2, POS, FEA...]
    psum x1 -> x0, blocking collectives: 76.4 us -> none  [body(): lax.psum(jnp.sum(owner * proxy[..., None], axis=(0, 1)), ('seq', 'tensor'))]
    reduce_scatter x1 -> x0, waiting for transfers between devices: 49.9 us -> none  [body(): lax.psum_scatter(partial_value.astype(jnp.bfloat16), 'tensor', scatter_di...]
    reduce_sum x37 -> x0, other arithmetic: 36.7 us -> none  [the longest x16 29.5 us: one_block(): totals = totals * rescale + jnp.sum(weights, axis=4)]
    add x34 -> x0, other arithmetic: 20.7 us -> none  [the longest x16 20.7 us: one_block(): totals = totals * rescale + jnp.sum(weights, axis=4)]
  transfers between devices with their start and end apart: 4 -> 0, of which waited for: 4 -> 0; matrix products, arithmetic and copies ran while one was open for 4% -> 0% of each run, Pallas kernels for 0% -> 0%
where the time goes in v2:
time: 157 us; the launch traced here: 156 us
  Pallas kernels  149 us (95%)
  local copies, waits for them, and re-layouts  6.54 us (4%)
    pallas_call x1, Pallas kernels, body(): pl.pallas_call(block_kernel, out_shape=(jax.ShapeDtypeStruct((2, POS, FEA...  149 us
    unnamed x2, local copies, waits for them, and re-layouts  4.02 us

profile of v2, /device:TPU:1, one launch (start us, length us, event | category | flops | bytes accessed | tf_op | source)
XLA Modules:
  0.0 156.3 jit_solution(13596705529107209262)
XLA Ops:
  0.6 1.3 broadcast_in_dim.3.gain
  2.0 2.0 %copy.12.hidden = bf16[2,256,448]{2,1,0:T(8,128)(2,1)} copy(bf16[2,256,448]{1,2,0:T(8,128)(2,1)} %param.10) | data formatting | bytes 917504 | tf_op args[0]
  4.0 149.1 %block.1 = (bf16[2,256,448]{2,1,0:T(8,128)(2,1)}, f32[8,128]{1,0:T(8,128)}) custom-call(bf16[2,256,448]{2,1,0:T(8,128)(2,1)} %copy.12.hidden, bf16[512,448]{1,0:T(8,128)(2,1)} %bitcast.3, f32[1,3584]{1,0:T(1,128)} %broadcast_in_dim.3.gain, bf16[3584,1152]{1,0:T(8,128)(2,1)} %w.1, bf16[28,3584]{1,0:T(8,128)(2,1)} %w_out.1, s32[2,16]{1,0:T(2,128)} %lengths.1, ...), custom_call_target="tpu_custom_call" | custom-call | flops 20000000000 | bytes 20000000 | tf_op jit(solution)/shard_map/block/pallas_call | solution.py:615
  153.1 2.0 %copy.13 = bf16[2,256,448]{1,2,0:T(8,128)(2,1)} copy(bf16[2,256,448]{2,1,0:T(8,128)(2,1)} %get-tuple-element.6) | data formatting | bytes 917504
  155.1 1.2 slice_bitcast_fusion

commit v3 on v2

--- a/solution.py
+++ b/solution.py
@@ -22,11 +22,13 @@
 HALF = POS // 2
 WIDE = 2 * FEAT
 SUB = HALF // 2
+PIECES = 2
+PIECE = SUB // PIECES
 COLS = (GROUP + 2) * HEAD_DIM
 SHARD = 28
 SLOT = 32
 DEPTH = SEQ * SLOT
-WINDOW = 9
+REACH = 17
 QSCALE = HEAD_DIM**-0.5 * 1.4426950408889634
 LOW = -1e30
 MESH = pl.DeviceIdType.MESH
@@ -67,25 +69,26 @@
         self.z = place()[1]
         self.peers = ring_peers()
 
-    def piece(self, way, hop, sub, mine):
+    def piece(self, way, hop, at, mine):
         step = 1 if way == 0 else RING - 1
         origin = lax.rem(self.z + (RING - step) * (hop - 1 if mine else hop), RING)
-        rows = pl.ds(sub * SUB, SUB)
+        rows = pl.ds(at * PIECE, PIECE)
         src = self.x.at[rows] if mine and hop == 1 else self.buf.at[origin, rows]
-        index = (way, hop - 1, sub)
+        index = (way, hop - 1, at)
         return push(src, self.buf.at[origin, rows], self.send.at[index], self.recv.at[index], self.peers[way])
 
     def start(self):
-        for sub in range(2):
+        for at in range(2 * PIECES):
             for way in range(2):
-                self.piece(way, 1, sub, True).start()
+                self.piece(way, 1, at, True).start()
 
     def relay(self, hop, sub):
-        for way in range(2):
-            if hop < 4 or sub == way:
-                self.piece(way, hop, sub, False).wait_recv()
-            if hop < 3 or (hop == 3 and sub == way):
-                self.piece(way, hop + 1, sub, True).start()
+        for at in range(sub * PIECES, (sub + 1) * PIECES):
+            for way in range(2):
+                if hop < 4 or sub == way:
+                    self.piece(way, hop, at, False).wait_recv()
+                if hop < 3 or (hop == 3 and sub == way):
+                    self.piece(way, hop + 1, at, True).start()
 
     def block(self, away):
         origin = lax.rem(self.z + away, RING)
@@ -93,10 +96,10 @@
 
     def drain(self):
         for hop in range(1, 5):
-            for sub in range(2):
+            for at in range(2 * PIECES):
                 for way in range(2):
-                    if hop < 4 or sub == way:
-                        self.piece(way, hop, sub, True).wait_send()
+                    if hop < 4 or at // PIECES == way:
+                        self.piece(way, hop, at, True).wait_send()
 
 
 class Projection:
@@ -242,45 +245,83 @@
             self.await_(self.slots[a, 2], "s2", a, BACK[way], way)
         self.go("sib", a, 2, 0)
 
-    def finish(self):
-        for a in range(4):
-            for b in range(4):
-                self.await_(self.theirs[a, b], "sib", a, b, 0)
-        self.keep().wait()
+    def handed(self, *blocks):
+        for a, b in blocks:
+            self.await_(self.theirs[a, b], "sib", a, b, 0)
 
     def drain(self):
         for key in self.sent:
             self.move(key).wait_send()
 
-    def steps(self):
-        cross, far = self.cross, self.far
-        return [
-            self.first_hop, lambda: cross(0), self.second_hop, lambda: cross(3), lambda: cross(1),
-            lambda: far(0), lambda: cross(2), lambda: far(3), lambda: far(1), lambda: far(2),
-        ]
-
-
-def attend(step, q, kv, begin, acc, top):
+    def mine(self):
+        self.keep().wait()
+        self.handed((0, 0))
+
+    def near(self):
+        self.first_hop()
+        self.cross(0)
+        self.handed((3, 0), (1, 0), (0, 3), (0, 1))
+
+    def corners(self):
+        self.cross(3)
+        self.cross(1)
+        self.far(0)
+        self.handed((3, 3), (3, 1), (1, 3), (1, 1), (2, 0), (0, 2))
+
+    def wings(self):
+        self.far(3)
+        self.far(1)
+
+    def rest(self):
+        self.far(2)
+        self.handed((2, 1), (2, 3), (1, 2), (3, 2), (2, 2))
+
+    def rest_of(self):
+        self.far(2)
+        self.handed(*((a, b) for a in range(4) for b in range(4)))
+        self.keep().wait()
+
+
+VISITS = (
+    (0, 0), (0, 3), (3, 0), (0, 1), (1, 0),
+    (3, 3), (3, 1), (2, 0), (0, 2), (1, 3), (1, 1),
+    (2, 3), (3, 2), (2, 1), (1, 2), (2, 2),
+)
+
+
+def visit(n):
     s, _ = place()
-    last = s - 2 * step
-    low = jnp.maximum(last - 1, 0)
+    x, y = s // 8, lax.rem(s // 2, 4)
+    dx, dy = jnp.int32(0), jnp.int32(0)
+    for at, (stepx, stepy) in enumerate(VISITS):
+        dx = dx + jnp.where(n == at, stepx, 0)
+        dy = dy + jnp.where(n == at, stepy, 0)
+    chip = lax.rem(x + dx, 4) * 4 + lax.rem(y + dy, 4)
+    return chip, (2 * chip <= s) & (2 * chip + 1 >= s - REACH)
+
+
+def attend(chip, q, kv, begin, acc, top, scores_ref, weights):
+    s, _ = place()
+    low = 2 * chip
     key_pos = low * POS + lax.broadcasted_iota(jnp.int32, (POS, 2 * POS), 1)
     query_pos = s * POS + lax.broadcasted_iota(jnp.int32, (POS, 2 * POS), 0)
-    allowed = (key_pos >= jnp.concatenate([begin] * 4, axis=1)) & (key_pos <= jnp.minimum(query_pos, last * POS + POS - 1))
+    allowed = (key_pos >= jnp.concatenate([begin] * 4, axis=1)) & (key_pos <= query_pos)
     bias = jnp.where(allowed, 0.0, LOW)
     blocks = kv[pl.ds(low, 2)]
     keys = jnp.concatenate([blocks[0, :HEAD_DIM], blocks[1, :HEAD_DIM]], axis=1)
     values = [blocks[n, HEAD_DIM:, m * HEAD_DIM : (m + 1) * HEAD_DIM] for n in (0, 1) for m in (0, 1)]
     values = jnp.concatenate(values, axis=0)
     values = jnp.concatenate([values, jnp.ones_like(values)], axis=1)
+    scores_ref[...] = dot(q[...].reshape(GROUP * POS, HEAD_DIM), keys)
     for n in range(GROUP):
-        scores = dot(q[n], keys) + bias
+        rows = slice(n * POS, (n + 1) * POS)
+        scores = scores_ref[rows] + bias
         old = top[n]
         new = jnp.maximum(old, jnp.max(scores, axis=1, keepdims=True))
-        weights = jnp.exp2(scores - jnp.concatenate([new] * 4, axis=1)).astype(BF16)
-        rescale = jnp.exp2(old - new)
-        acc[n] = acc[n] * jnp.concatenate([rescale] * 2, axis=1) + dot(weights, values)
+        weights[rows] = jnp.exp2(scores - jnp.concatenate([new] * 4, axis=1)).astype(BF16)
+        acc[n] = acc[n] * jnp.concatenate([jnp.exp2(old - new)] * 2, axis=1)
         top[n] = new
+    acc[...] = acc[...] + dot(weights[...], values).reshape(GROUP, POS, 2 * HEAD_DIM)
 
 
 def finish_attend(acc, ctx):
@@ -305,106 +346,105 @@
         product = jnp.where(odd == 1, product[:, 64:], product[:, :FEAT])
         return pack(product)
 
-    def move(self, way, k, sub):
-        rows = pl.ds(sub * SUB, SUB)
-        index = (way, k, sub)
+    def move(self, way, k, at):
+        rows = pl.ds(at * PIECE, PIECE)
+        index = (way, k, at)
         return push(
             self.out.at[way, k, rows], self.came.at[way, k, rows],
             self.send.at[index], self.recv.at[index], self.peers[way],
         )
 
-    def ship(self, way, k, sub, value):
-        self.out[way, k, pl.ds(sub * SUB, SUB)] = value.astype(BF16)
-        self.move(way, k, sub).start()
-
-    def arrived(self, way, k, sub):
-        self.move(way, k, sub).wait_recv()
-        return self.came[way, k, pl.ds(sub * SUB, SUB)].astype(F32)
+    def ship(self, way, k, at, value):
+        self.out[way, k, pl.ds(at * PIECE, PIECE)] = value.astype(BF16)
+        self.move(way, k, at).start()
+
+    def arrived(self, way, k, at):
+        self.move(way, k, at).wait_recv()
+        return self.came[way, k, pl.ds(at * PIECE, PIECE)].astype(F32)
 
     def first(self):
         value = self.part(4)
-        for way in range(2):
-            self.ship(way, 0, way, value[way * SUB : (way + 1) * SUB])
+        for at in range(2 * PIECES):
+            self.ship(at // PIECES, 0, at, value[at * PIECE : (at + 1) * PIECE])
 
     def ready(self, k):
         self.parts[0] = self.part(4 - k)
         self.parts[1] = self.part(4 + k)
 
     def turn(self, k, turn):
-        for way in range(2):
-            sub = 1 - (turn ^ way) if k == 1 else turn
-            piece = self.parts[way, pl.ds(sub * SUB, SUB)]
-            if k > 1 or sub == way:
-                piece = piece + self.arrived(way, k - 1, sub)
-            self.ship(way, k, sub, piece)
+        for n in range(PIECES):
+            for way in range(2):
+                sub = 1 - (turn ^ way) if k == 1 else turn
+                at = sub * PIECES + n
+                piece = self.parts[way, pl.ds(at * PIECE, PIECE)]
+                if k > 1 or sub == way:
+                    piece = piece + self.arrived(way, k - 1, at)
+                self.ship(way, k, at, piece)
 
     def finish(self):
         self.parts[0] = self.part(0)
-        for sub in range(2):
-            rows = pl.ds(sub * SUB, SUB)
-            self.parts[0, rows] = self.parts[0, rows] + self.arrived(0, 3, sub) + self.arrived(1, 3, sub)
+        for at in range(2 * PIECES):
+            rows = pl.ds(at * PIECE, PIECE)
+            self.parts[0, rows] = self.parts[0, rows] + self.arrived(0, 3, at) + self.arrived(1, 3, at)
 
     def drain(self):
         for way in range(2):
             for k in range(4):
-                for sub in range(2):
-                    if k > 0 or sub == way:
-                        self.move(way, k, sub).wait_send()
-
-    def steps(self):
-        def both(k):
-            self.ready(k)
-            self.turn(k, 0)
-
-        return [
-            self.first,
-            lambda: both(1), lambda: self.turn(1, 1),
-            lambda: both(2), lambda: self.turn(2, 1),
-            lambda: both(3), lambda: self.turn(3, 1),
-        ]
-
-
-def emit(delta, x, owner, out):
-    delta = unpack(delta)
-    out[...] = (unpack(x).astype(F32) + delta).astype(BF16)
+                for at in range(2 * PIECES):
+                    if k > 0 or at // PIECES == way:
+                        self.move(way, k, at).wait_send()
+
+    def both(self, k):
+        self.ready(k)
+        self.turn(k, 0)
+
+
+def losses(delta, owner):
     proxy = jnp.sum(delta * delta, axis=1, keepdims=True) / D
     lanes = lax.broadcasted_iota(jnp.int32, (POS, HEAD_DIM), 1)
-    total = jnp.sum(jnp.where(owner[...] == lanes, proxy, 0.0), axis=0, keepdims=True)
+    total = jnp.sum(jnp.where(owner == lanes, proxy, 0.0), axis=0, keepdims=True)
     return jnp.broadcast_to(total, (8, HEAD_DIM))
+
+
+def emit(delta, x, out):
+    out[...] = (unpack(x).astype(F32) + delta).T.astype(BF16)
 
 
 def loss_groups():
     s, z = place()
-    x, y, c = s // 8, lax.rem(s // 2, 4), lax.rem(s, 2)
-    xc = x * 2 + c
+    chip, c = s // 2, lax.rem(s, 2)
     return [
-        (z, 8, lambda n: (s, n)),
-        (xc, 8, lambda n: ((n // 2) * 8 + y * 2 + lax.rem(n, 2), z)),
-        (y, 4, lambda n: (x * 8 + n * 2 + c, z)),
+        (z * 2 + c, lambda n: (2 * chip + lax.rem(n, 2), n // 2)),
+        (chip, lambda n: (2 * n + c, z)),
     ]
 
 
 def loss_peers():
-    return [who(lax.rem(me + j, n)) for me, n, who in loss_groups() for j in range(1, n)]
-
-
-def loss_total(value, slots, send, recv):
-    for stage, (me, n, who) in enumerate(loss_groups()):
+    return [who(lax.rem(me + j, 16)) for me, who in loss_groups() for j in range(1, 16)]
+
+
+def loss_total(value, slots, send, recv, between):
+    copies = []
+    for stage, (me, who) in enumerate(loss_groups()):
         slots[stage, me] = value
-        sent = []
-        for j in range(1, n):
-            ref = slots.at[stage, me]
-            copy = push(ref, ref, send.at[stage, j], recv.at[stage, j], who(lax.rem(me + j, n)))
+
+        def swap(j, origin):
+            ref = slots.at[stage, origin]
+            return push(ref, ref, send.at[stage, j], recv.at[stage, j], who(lax.rem(me + j, 16)))
+
+        for j in range(1, 16):
+            copy = swap(j, me)
             copy.start()
-            sent.append(copy)
-        for j in range(1, n):
-            ref = slots.at[stage, lax.rem(me + n - j, n)]
-            push(ref, ref, send.at[stage, j], recv.at[stage, j], who(lax.rem(me + j, n))).wait_recv()
+            copies.append(copy)
+        if stage == 0:
+            between()
+        for j in range(1, 16):
+            swap(j, lax.rem(me + 16 - j, 16)).wait_recv()
         value = slots[stage, 0]
-        for j in range(1, n):
+        for j in range(1, 16):
             value = value + slots[stage, j]
-        for copy in sent:
-            copy.wait_send()
+    for copy in copies:
+        copy.wait_send()
     return value
 
 
@@ -433,17 +473,17 @@
     picker = jnp.where(jnp.concatenate([slot] * 4, axis=1) == entries, 1.0, 0.0).astype(BF16)
     lookup = dot(picker, table[...])
     left = jnp.concatenate([prompt - within] * 4, axis=1)[:, :FEAT]
-    x[row] = pack(jnp.where(left > 0, lookup, hidden[row].astype(F32)).astype(BF16))
+    x[row] = pack(jnp.where(left > 0, lookup, hidden[row].astype(F32).T).astype(BF16))
 
 
 def block_kernel(
-    hidden, table, gain, w, w_out, lengths, tenants, prompts, freq, perm,
+    hidden_any, table_any, gain, w, w_out, lengths, tenants, prompts, freq,
     out, loss,
-    x, begin, within, owner, cos, sin, gains,
+    hidden, table, hsem, x, begin, within, owner, cos, sin, gains,
     wbuf, wsem, acc, ssq, buf0, buf1, fsend0, frecv0, fsend1, frecv1,
     q, own, keys0, keys1, ksend0, krecv0, ksend1, krecv1, klocal,
-    wpad, wall, osend, orecv, olocal, permbuf, psem,
-    total, top, ctx, mixed, parts,
+    wpad, wall, osend, orecv, olocal, permbuf,
+    total, top, scores, weights_bf, ctx, mixed, parts,
     sout0, came0, ssend0, srecv0, sout1, came1, ssend1, srecv1,
     slots, lsend, lrecv,
 ):
@@ -452,16 +492,20 @@
     barrier = pltpu.get_barrier_semaphore()
     for peer in peers:
         pl.semaphore_signal(barrier, inc=1, device_id=peer, device_id_type=MESH)
+    arriving = [pltpu.make_async_copy(hidden_any, hidden, hsem.at[0]), pltpu.make_async_copy(table_any, table, hsem.at[1])]
+    for copy in arriving:
+        copy.start()
     proj = Projection(gains, w, wbuf, wsem, acc, ssq)
     proj.fetch()
-    perm_copy = pltpu.make_async_copy(perm, permbuf, psem)
-    perm_copy.start()
     doc_refs = (lengths, tenants, prompts)
+    for copy in arriving:
+        copy.wait()
     embed(0, hidden, table, *doc_refs, x, begin, within, owner)
     wpad[:SHARD] = w_out[...]
     wpad[SHARD:] = jnp.zeros((SLOT - SHARD, D), BF16)
+    whole = jnp.concatenate([gain[n : n + 1] for n in range(D // 128)], axis=1)
     for n in range(RING):
-        gains[n] = gain[:, n * FEAT : (n + 1) * FEAT]
+        gains[n] = whole[:, n * FEAT : (n + 1) * FEAT]
     pl.semaphore_wait(barrier, len(peers))
 
     ring = [Ring(x.at[0], buf0, fsend0, frecv0), Ring(x.at[1], buf1, fsend1, frecv1)]
@@ -471,9 +515,16 @@
         Plane(own.at[1], keys1, ksend1, krecv1, klocal.at[1]),
     ]
     sums = [
-        Sums(wall, mixed, parts, sout0, came0, ssend0, srecv0),
-        Sums(wall, mixed, parts, sout1, came1, ssend1, srecv1),
+        Sums(wall, mixed.at[0], parts.at[0], sout0, came0, ssend0, srecv0),
+        Sums(wall, mixed.at[1], parts.at[1], sout1, came1, ssend1, srecv1),
     ]
+
+    def spacing():
+        column = lax.broadcasted_iota(jnp.int32, (GROUP * HEAD_DIM, DEPTH), 1)
+        row = lax.broadcasted_iota(jnp.int32, (GROUP * HEAD_DIM, DEPTH), 0)
+        inside = column & (SLOT - 1)
+        hit = (row == (column >> 5) * SHARD + inside) & (inside < SHARD)
+        permbuf[...] = jnp.where(hit, 1.0, 0.0).astype(BF16)
 
     def angles(row):
         angle = within[row].astype(F32) * freq[...]
@@ -482,92 +533,131 @@
         sine = jnp.sin(angle)
         sin[row] = jnp.where(lane < HEAD_DIM // 2, -sine, sine)
 
-    def gather(row, between):
-        between = list(between)
-
-        def other(n=1):
-            for _ in range(n):
-                if between:
-                    between.pop(0)()
-
-        proj.absorb(x[row], place()[1], row == 0, True)
-        other()
-        for hop in range(1, 4):
-            ring[row].relay(hop, 0)
-            other()
-            ring[row].relay(hop, 1)
-            other()
-            if hop == 3 and row == 0:
-                ring[1].start()
-            proj.absorb(*ring[row].block(RING - hop), row == 0, False)
-            other()
-            proj.absorb(*ring[row].block(hop), row == 0, False)
-        for sub in range(2):
-            ring[row].relay(4, sub)
-        proj.absorb(*ring[row].block(4), row == 0, False)
-        return between
-
-    def queries_keys(row):
+    def absorb(row, *steps):
+        for away in steps:
+            proj.absorb(*ring[row].block(away), row == 0, False)
+
+    def projected(row):
         queries = proj.finish(cos.at[row], sin.at[row], q.at[row], own.at[row])
         keys[row].start()
         queries()
 
-    def attention(row, between):
+    def attention(row, beside):
         total[...] = jnp.zeros_like(total)
         top[...] = jnp.full_like(top, LOW)
         everyone = (keys0, keys1)[row]
 
         def step(n, carry):
-            @pl.when(s >= 2 * n)
+            for at, steps in beside.items():
+
+                @pl.when(n == at)
+                def _(steps=steps):
+                    for one in steps:
+                        one()
+
+            chip, useful = visit(n)
+
+            @pl.when(useful)
             def _():
-                attend(n, q.at[row], everyone, begin[row], total, top)
-
-            for at, one in enumerate(between):
-                pl.when(n == at)(one)
+                attend(chip, q.at[row], everyone, begin[row], total, top, scores, weights_bf)
+
             return carry
 
-        lax.fori_loop(0, WINDOW, step, 0)
+        lax.fori_loop(0, len(VISITS), step, 0)
         finish_attend(total, ctx)
+        mixed[row] = dot(ctx[...], permbuf[...]).astype(BF16)
 
     ring[0].start()
     weights.start()
+    proj.absorb(x[0], place()[1], True, True)
     embed(1, hidden, table, *doc_refs, x, begin, within, owner)
+    ring[0].relay(1, 0)
     angles(0)
-    rest = gather(0, weights.steps()[:6] + [lambda: angles(1)])
-    queries_keys(0)
-    rest = rest + weights.steps()[6:]
-    gather_steps = keys[0].steps()
-    rest = gather(1, gather_steps[:6] + rest + gather_steps[6:])
-    queries_keys(1)
-    for one in rest:
-        one()
-    keys[0].finish()
-
-    key_steps = keys[1].steps()
-    attention(0, key_steps[:8] + [lambda: (key_steps[8](), key_steps[9]()) and None])
-    weights.finish()
-    keys[1].finish()
-    perm_copy.wait()
-    mixed[...] = dot(ctx[...], permbuf[...]).astype(BF16)
-    attention(1, sums[0].steps())
-    sums[0].finish()
-    share = emit(parts[0], x[0], owner.at[0], out.at[0])
-    mixed[...] = dot(ctx[...], permbuf[...]).astype(BF16)
-    for one in sums[1].steps():
-        one()
-    sums[1].finish()
-    share = share + emit(parts[0], x[1], owner.at[1], out.at[1])
-    loss[...] = loss_total(share, slots, lsend, lrecv)
-    for one in ring + [weights] + keys + sums:
-        one.drain()
+    ring[0].relay(1, 1)
+    weights.first_hop()
+    weights.cross(0)
+    absorb(0, 7, 1)
+    ring[0].relay(2, 0)
+    spacing()
+    ring[0].relay(2, 1)
+    weights.second_hop()
+    absorb(0, 6, 2)
+    ring[0].relay(3, 0)
+    weights.cross(3)
+    ring[0].relay(3, 1)
+    ring[1].start()
+    weights.cross(1)
+    absorb(0, 5, 3)
+    angles(1)
+    weights.far(0)
+    ring[0].relay(4, 0)
+    ring[0].relay(4, 1)
+    absorb(0, 4)
+    projected(0)
+    ring[1].relay(1, 0)
+    weights.cross(2)
+
+    k0, k1, w_, r = keys[0], keys[1], weights, ring[1]
+    attention(0, {
+        0: [k0.mine],
+        1: [
+            lambda: r.relay(1, 1), lambda: proj.absorb(x[1], place()[1], False, True),
+            lambda: absorb(1, 7, 1), lambda: r.relay(2, 0), k0.near,
+        ],
+        3: [lambda: r.relay(2, 1), k0.second_hop],
+        4: [lambda: absorb(1, 6, 2), lambda: r.relay(3, 0)],
+        5: [k0.corners],
+        6: [lambda: r.relay(3, 1), lambda: k0.cross(2)],
+        7: [lambda: absorb(1, 5, 3), lambda: r.relay(4, 0), lambda: r.relay(4, 1),
+            lambda: absorb(1, 4), lambda: projected(1)],
+        8: [w_.wings],
+        9: [k0.wings],
+        11: [k0.rest],
+        12: [w_.rest_of],
+    })
+    one, other = sums
+    one.first()
+    attention(1, {
+        0: [k1.mine, lambda: one.both(1)],
+        1: [k1.near],
+        2: [lambda: one.turn(1, 1)],
+        3: [k1.second_hop],
+        4: [lambda: one.both(2)],
+        5: [k1.corners],
+        6: [lambda: k1.cross(2)],
+        7: [lambda: one.turn(2, 1)],
+        9: [lambda: one.both(3), k1.wings],
+        11: [k1.rest],
+        12: [lambda: one.turn(3, 1)],
+    })
+    other.first()
+    other.both(1)
+    one.finish()
+    other.turn(1, 1)
+    delta = unpack(one.parts[0])
+    share = losses(delta, owner[0])
+    emit(delta, x[0], out.at[0])
+    for k in range(2, 4):
+        other.both(k)
+        other.turn(k, 1)
+    other.finish()
+    delta = unpack(other.parts[0])
+    share = share + losses(delta, owner[1])
+    result = loss_total(share, slots, lsend, lrecv, lambda: emit(delta, x[1], out.at[1]))
+    loss[...] = result[:1, :TENANTS]
+    for each in ring + [weights] + keys + sums:
+        each.drain()
 
 
 DMA = pltpu.SemaphoreType.DMA
-RING_SEMS = DMA((2, 4, 2))
+RING_SEMS = DMA((2, 4, 2 * PIECES))
 VM = pl.BlockSpec(memory_space=pltpu.VMEM)
 SM = pl.BlockSpec(memory_space=pltpu.SMEM)
 ANY = pl.BlockSpec(memory_space=pl.ANY)
 SCRATCH = [
+    pltpu.VMEM((2, FEAT, POS), BF16),
+    pltpu.VMEM((TENANTS * PLEN, FEAT), BF16),
+    DMA((2,)),
     pltpu.VMEM((2, HALF, WIDE), BF16),
     pltpu.VMEM((2, POS, HEAD_DIM), jnp.int32),
     pltpu.VMEM((2, POS, HEAD_DIM), jnp.int32),
@@ -592,30 +682,28 @@
     pltpu.VMEM((SEQ, SLOT, D), BF16),
     DMA((KEY_SEMS,)), DMA((KEY_SEMS,)), DMA,
     pltpu.VMEM((GROUP * HEAD_DIM, DEPTH), BF16),
-    DMA,
     pltpu.VMEM((GROUP, POS, 2 * HEAD_DIM), F32),
     pltpu.VMEM((GROUP, POS, HEAD_DIM), F32),
+    pltpu.VMEM((GROUP * POS, 4 * HEAD_DIM), F32),
+    pltpu.VMEM((GROUP * POS, 4 * HEAD_DIM), BF16),
     pltpu.VMEM((POS, GROUP * HEAD_DIM), BF16),
-    pltpu.VMEM((POS, DEPTH), BF16),
-    pltpu.VMEM((2, HALF, WIDE), F32),
+    pltpu.VMEM((2, POS, DEPTH), BF16),
+    pltpu.VMEM((2, 2, HALF, WIDE), F32),
     pltpu.VMEM((2, 4, HALF, WIDE), BF16), pltpu.VMEM((2, 4, HALF, WIDE), BF16), RING_SEMS, RING_SEMS,
     pltpu.VMEM((2, 4, HALF, WIDE), BF16), pltpu.VMEM((2, 4, HALF, WIDE), BF16), RING_SEMS, RING_SEMS,
-    pltpu.VMEM((3, RING, 8, HEAD_DIM), F32),
-    DMA((3, RING)),
-    DMA((3, RING)),
+    pltpu.VMEM((2, 16, 8, HEAD_DIM), F32),
+    DMA((2, 16)),
+    DMA((2, 16)),
 ]
 
 
 def body(hidden_in, prompt_table, norm_gain, w_qkv, w_out, doc_lengths, doc_tenant, prompt_lengths):
     freq = THETA ** (-np.arange(HEAD_DIM // 2) / (HEAD_DIM // 2))
     freq = jnp.asarray(np.concatenate([freq, freq])[None], F32)
-    rows = np.arange(GROUP * HEAD_DIM)
-    perm = np.zeros((GROUP * HEAD_DIM, DEPTH), np.float32)
-    perm[rows, rows // SHARD * SLOT + rows % SHARD] = 1
     out, loss = pl.pallas_call(
         block_kernel,
-        out_shape=(jax.ShapeDtypeStruct((2, POS, FEAT), BF16), jax.ShapeDtypeStruct((8, HEAD_DIM), F32)),
-        in_specs=[VM, VM, VM, ANY, VM, SM, SM, SM, VM, ANY],
+        out_shape=(jax.ShapeDtypeStruct((2, FEAT, POS), BF16), jax.ShapeDtypeStruct((1, TENANTS), F32)),
+        in_specs=[ANY, ANY, VM, ANY, VM, SM, SM, SM, VM],
         out_specs=(VM, VM),
         scratch_shapes=SCRATCH,
         compiler_params=pltpu.CompilerParams(
@@ -624,10 +712,10 @@
         cost_estimate=pl.CostEstimate(flops=2 * 10**10, bytes_accessed=2 * 10**7, transcendentals=10**7),
         name="block",
     )(
-        hidden_in, prompt_table.reshape(TENANTS * PLEN, FEAT), norm_gain[None], w_qkv, w_out,
-        doc_lengths, doc_tenant, prompt_lengths, freq, jnp.asarray(perm, BF16),
+        jnp.transpose(hidden_in, (0, 2, 1)), prompt_table.reshape(TENANTS * PLEN, FEAT), norm_gain.reshape(D // 128, 128), w_qkv, w_out,
+        doc_lengths, doc_tenant, prompt_lengths, freq,
     )
-    return out, loss[0, :TENANTS]
+    return jnp.transpose(out, (0, 2, 1)), loss.reshape(TENANTS)
 
 
 def solution(mesh):

time: 157 us -> 133 us (0.85)
  Pallas kernels: 149 us -> 130 us
  local copies, waits for them, and re-layouts: 6.54 us -> 3.01 us
    pallas_call x1, Pallas kernels: 149 us -> 130 us  [body(): pl.pallas_call(block_kernel, out_shape=(jax.ShapeDtypeStruct((2, FEAT, PO...]
where the time goes in v3:
time: 133 us
  Pallas kernels  130 us (98%)
  local copies, waits for them, and re-layouts  3.01 us (2%)
    pallas_call x1, Pallas kernels, body(): pl.pallas_call(block_kernel, out_shape=(jax.ShapeDtypeStruct((2, FEAT, PO...  130 us
    unnamed x2, local copies, waits for them, and re-layouts  3.01 us

profile of v3, /device:TPU:1, one launch (start us, length us, event | category | flops | bytes accessed | tf_op | source)
XLA Modules:
  0.0 133.3 jit_solution(2986309011164442340)
XLA Ops:
  0.6 129.7 %block.1 = (bf16[2,448,256]{2,1,0:T(8,128)(2,1)}, f32[1,16]{1,0:T(1,128)}) custom-call(bf16[2,448,256]{2,1,0:T(8,128)(2,1)} %bitcast.7, bf16[512,448]{1,0:T(8,128)(2,1)} %bitcast.6, f32[28,128]{1,0:T(8,128)} %bitcast.8, bf16[3584,1152]{1,0:T(8,128)(2,1)} %w.1, bf16[28,3584]{1,0:T(8,128)(2,1)} %w_out.1, s32[2,16]{1,0:T(2,128)} %lengths.1, s32[2,16]{1,0:T(2,128)} %tenants.1, ...), custom_call_target="tpu_custom_call" | custom-call | flops 20000000000 | bytes 20000000 | tf_op jit(solution)/shard_map/block/pallas_call | solution.py:703
  130.3 1.8 %copy.13 = bf16[2,256,448]{1,2,0:T(8,128)(2,1)} copy(bf16[2,256,448]{1,2,0:T(8,128)(2,1)} %bitcast.5) | data formatting | bytes 917504
  132.1 1.2 copy.14

commit v4 on v3

--- a/solution.py
+++ b/solution.py
@@ -297,31 +297,32 @@
         dx = dx + jnp.where(n == at, stepx, 0)
         dy = dy + jnp.where(n == at, stepy, 0)
     chip = lax.rem(x + dx, 4) * 4 + lax.rem(y + dy, 4)
-    return chip, (2 * chip <= s) & (2 * chip + 1 >= s - REACH)
-
-
-def attend(chip, q, kv, begin, acc, top, scores_ref, weights):
+    inside = [(2 * chip + c <= s) & (2 * chip + c >= s - REACH) for c in range(2)]
+    return chip, inside[0], inside[1]
+
+
+def attend(low, count, q, kv, begin, acc, top, scores_ref, weights):
     s, _ = place()
-    low = 2 * chip
-    key_pos = low * POS + lax.broadcasted_iota(jnp.int32, (POS, 2 * POS), 1)
-    query_pos = s * POS + lax.broadcasted_iota(jnp.int32, (POS, 2 * POS), 0)
-    allowed = (key_pos >= jnp.concatenate([begin] * 4, axis=1)) & (key_pos <= query_pos)
+    span = count * POS
+    key_pos = low * POS + lax.broadcasted_iota(jnp.int32, (POS, span), 1)
+    query_pos = s * POS + lax.broadcasted_iota(jnp.int32, (POS, span), 0)
+    allowed = (key_pos >= jnp.concatenate([begin] * (2 * count), axis=1)) & (key_pos <= query_pos)
     bias = jnp.where(allowed, 0.0, LOW)
-    blocks = kv[pl.ds(low, 2)]
-    keys = jnp.concatenate([blocks[0, :HEAD_DIM], blocks[1, :HEAD_DIM]], axis=1)
-    values = [blocks[n, HEAD_DIM:, m * HEAD_DIM : (m + 1) * HEAD_DIM] for n in (0, 1) for m in (0, 1)]
+    blocks = [kv[low + n] for n in range(count)]
+    keys = jnp.concatenate([block[:HEAD_DIM] for block in blocks], axis=1)
+    values = [block[HEAD_DIM:, m * HEAD_DIM : (m + 1) * HEAD_DIM] for block in blocks for m in (0, 1)]
     values = jnp.concatenate(values, axis=0)
     values = jnp.concatenate([values, jnp.ones_like(values)], axis=1)
-    scores_ref[...] = dot(q[...].reshape(GROUP * POS, HEAD_DIM), keys)
+    scores_ref[:, :span] = dot(q[...].reshape(GROUP * POS, HEAD_DIM), keys)
     for n in range(GROUP):
         rows = slice(n * POS, (n + 1) * POS)
-        scores = scores_ref[rows] + bias
+        scores = scores_ref[rows, :span] + bias
         old = top[n]
         new = jnp.maximum(old, jnp.max(scores, axis=1, keepdims=True))
-        weights[rows] = jnp.exp2(scores - jnp.concatenate([new] * 4, axis=1)).astype(BF16)
+        weights[rows, :span] = jnp.exp2(scores - jnp.concatenate([new] * (2 * count), axis=1)).astype(BF16)
         acc[n] = acc[n] * jnp.concatenate([jnp.exp2(old - new)] * 2, axis=1)
         top[n] = new
-    acc[...] = acc[...] + dot(weights[...], values).reshape(GROUP, POS, 2 * HEAD_DIM)
+    acc[...] = acc[...] + dot(weights[:, :span], values).reshape(GROUP, POS, 2 * HEAD_DIM)
 
 
 def finish_attend(acc, ctx):
@@ -438,12 +439,15 @@
             copies.append(copy)
         if stage == 0:
             between()
+        else:
+            for copy in copies[:15]:
+                copy.wait_send()
         for j in range(1, 16):
             swap(j, lax.rem(me + 16 - j, 16)).wait_recv()
         value = slots[stage, 0]
         for j in range(1, 16):
             value = value + slots[stage, j]
-    for copy in copies:
+    for copy in copies[15:]:
         copy.wait_send()
     return value
 
@@ -477,8 +481,9 @@
 
 
 def block_kernel(
-    hidden_any, table_any, gain, w, w_out, lengths, tenants, prompts, freq,
-    out, loss,
+    hidden_any, table_any, gain_any, w, w_out, lengths_any, tenants_any, prompts_any, freq_any,
+    out_any, loss_any,
+    gain, lengths, tenants, prompts, freq, out, loss, osem,
     hidden, table, hsem, x, begin, within, owner, cos, sin, gains,
     wbuf, wsem, acc, ssq, buf0, buf1, fsend0, frecv0, fsend1, frecv1,
     q, own, keys0, keys1, ksend0, krecv0, ksend1, krecv1, klocal,
@@ -492,7 +497,11 @@
     barrier = pltpu.get_barrier_semaphore()
     for peer in peers:
         pl.semaphore_signal(barrier, inc=1, device_id=peer, device_id_type=MESH)
-    arriving = [pltpu.make_async_copy(hidden_any, hidden, hsem.at[0]), pltpu.make_async_copy(table_any, table, hsem.at[1])]
+    sources = (lengths_any, tenants_any, prompts_any, hidden_any, table_any, gain_any, freq_any)
+    targets = (lengths, tenants, prompts, hidden, table, gain, freq)
+    arriving = [
+        pltpu.make_async_copy(src, dst, hsem.at[n]) for n, (src, dst) in enumerate(zip(sources, targets))
+    ]
     for copy in arriving:
         copy.start()
     proj = Projection(gains, w, wbuf, wsem, acc, ssq)
@@ -555,11 +564,16 @@
                     for one in steps:
                         one()
 
-            chip, useful = visit(n)
-
-            @pl.when(useful)
+            chip, even, odd = visit(n)
+            state = (q.at[row], everyone, begin[row], total, top, scores, weights_bf)
+
+            @pl.when(even & odd)
             def _():
-                attend(chip, q.at[row], everyone, begin[row], total, top, scores, weights_bf)
+                attend(2 * chip, 2, *state)
+
+            @pl.when(even ^ odd)
+            def _():
+                attend(2 * chip + jnp.where(odd, 1, 0), 1, *state)
 
             return carry
 
@@ -637,27 +651,51 @@
     delta = unpack(one.parts[0])
     share = losses(delta, owner[0])
     emit(delta, x[0], out.at[0])
-    for k in range(2, 4):
-        other.both(k)
-        other.turn(k, 1)
+    leaving = [pltpu.make_async_copy(out.at[n], out_any.at[n], osem.at[n]) for n in range(2)]
+    leaving.append(pltpu.make_async_copy(loss, loss_any, osem.at[2]))
+    leaving[0].start()
+    for each in ring:
+        each.drain()
+    other.both(2)
+    weights.drain()
+    other.turn(2, 1)
+    for each in keys:
+        each.drain()
+    other.both(3)
+    one.drain()
+    other.turn(3, 1)
     other.finish()
     delta = unpack(other.parts[0])
     share = share + losses(delta, owner[1])
-    result = loss_total(share, slots, lsend, lrecv, lambda: emit(delta, x[1], out.at[1]))
+
+    def last_row():
+        emit(delta, x[1], out.at[1])
+        leaving[1].start()
+        other.drain()
+
+    result = loss_total(share, slots, lsend, lrecv, last_row)
     loss[...] = result[:1, :TENANTS]
-    for each in ring + [weights] + keys + sums:
-        each.drain()
+    leaving[2].start()
+    for copy in leaving:
+        copy.wait()
 
 
 DMA = pltpu.SemaphoreType.DMA
 RING_SEMS = DMA((2, 4, 2 * PIECES))
 VM = pl.BlockSpec(memory_space=pltpu.VMEM)
-SM = pl.BlockSpec(memory_space=pltpu.SMEM)
 ANY = pl.BlockSpec(memory_space=pl.ANY)
 SCRATCH = [
+    pltpu.VMEM((D // 128, 128), F32),
+    pltpu.SMEM((2, DOCS), jnp.int32),
+    pltpu.SMEM((2, DOCS), jnp.int32),
+    pltpu.SMEM((2, DOCS), jnp.int32),
+    pltpu.VMEM((1, HEAD_DIM), F32),
+    pltpu.VMEM((2, FEAT, POS), BF16),
+    pltpu.VMEM((1, TENANTS), F32),
+    DMA((3,)),
     pltpu.VMEM((2, FEAT, POS), BF16),
     pltpu.VMEM((TENANTS * PLEN, FEAT), BF16),
-    DMA((2,)),
+    DMA((7,)),
     pltpu.VMEM((2, HALF, WIDE), BF16),
     pltpu.VMEM((2, POS, HEAD_DIM), jnp.int32),
     pltpu.VMEM((2, POS, HEAD_DIM), jnp.int32),
@@ -697,14 +735,19 @@
 ]
 
 
+def pass_kernel(out, loss, out_again, loss_again):
+    out_again[...] = out[...]
+    loss_again[...] = loss[...]
+
+
 def body(hidden_in, prompt_table, norm_gain, w_qkv, w_out, doc_lengths, doc_tenant, prompt_lengths):
     freq = THETA ** (-np.arange(HEAD_DIM // 2) / (HEAD_DIM // 2))
     freq = jnp.asarray(np.concatenate([freq, freq])[None], F32)
     out, loss = pl.pallas_call(
         block_kernel,
         out_shape=(jax.ShapeDtypeStruct((2, FEAT, POS), BF16), jax.ShapeDtypeStruct((1, TENANTS), F32)),
-        in_specs=[ANY, ANY, VM, ANY, VM, SM, SM, SM, VM],
-        out_specs=(VM, VM),
+        in_specs=[ANY, ANY, ANY, ANY, VM, ANY, ANY, ANY, ANY],
+        out_specs=(ANY, ANY),
         scratch_shapes=SCRATCH,
         compiler_params=pltpu.CompilerParams(
             collective_id=1, has_side_effects=True, vmem_limit_bytes=60 * 2**20
@@ -715,6 +758,13 @@
         jnp.transpose(hidden_in, (0, 2, 1)), prompt_table.reshape(TENANTS * PLEN, FEAT), norm_gain.reshape(D // 128, 128), w_qkv, w_out,
         doc_lengths, doc_tenant, prompt_lengths, freq,
     )
+    out, loss = pl.pallas_call(
+        pass_kernel,
+        out_shape=(jax.ShapeDtypeStruct((2, FEAT, POS), BF16), jax.ShapeDtypeStruct((1, TENANTS), F32)),
+        in_specs=[VM, VM],
+        out_specs=(VM, VM),
+        name="hand_over",
+    )(out, loss)
     return jnp.transpose(out, (0, 2, 1)), loss.reshape(TENANTS)
 
 

time: 133 us -> 132 us (level)
  local copies, waits for them, and re-layouts: 3.01 us -> 0 us
    unnamed x2 -> x0, local copies, waits for them, and re-layouts: 3.01 us -> none
    pallas_call x0 -> x1, Pallas kernels: none -> 1.82 us  [body(): pl.pallas_call(pass_kernel, out_shape=(jax.ShapeDtypeStruct((2, FEAT, POS...]
where the time goes in v4:
time: 132 us
  Pallas kernels  131 us (99%)
    pallas_call x1, Pallas kernels, body(): pl.pallas_call(block_kernel, out_shape=(jax.ShapeDtypeStruct((2, FEAT, PO...  129 us

profile of v4, /device:TPU:1, one launch (start us, length us, event | category | flops | bytes accessed | tf_op | source)
XLA Modules:
  0.0 131.7 jit_solution(5553384840361878825)
XLA Ops:
  0.6 129.3 %block.1 = (bf16[2,448,256]{2,1,0:T(8,128)(2,1)}, f32[1,16]{1,0:T(1,128)}) custom-call(bf16[2,448,256]{2,1,0:T(8,128)(2,1)} %bitcast.6, bf16[512,448]{1,0:T(8,128)(2,1)} %bitcast.5, f32[28,128]{1,0:T(8,128)} %bitcast.8, bf16[3584,1152]{1,0:T(8,128)(2,1)} %w.1, bf16[28,3584]{1,0:T(8,128)(2,1)} %w_out.1, s32[2,16]{1,0:T(2,128)} %lengths_any.1, ...), custom_call_target="tpu_custom_call" | custom-call | flops 20000000000 | bytes 20000000 | tf_op jit(solution)/shard_map/block/pallas_call | solution.py:746
  129.9 1.8 %hand_over.1 = (bf16[2,448,256]{2,1,0:T(8,128)(2,1)}, f32[1,16]{1,0:T(1,128)}) custom-call(bf16[2,448,256]{2,1,0:T(8,128)(2,1)} %get-tuple-element.6.out, f32[1,16]{1,0:T(1,128)} %get-tuple-element.7.loss), custom_call_target="tpu_custom_call" | custom-call | tf_op jit(solution)/shard_map/hand_over/pallas_call | solution.py:761
